TPU v7x, 256 devices: a whole 4x4x8 slice. The times are simulated.
256 devices in a mesh: dom: 128 (over y, z, x_hi, core), rep: 2 (over x_lo).
Axes of the slice: x: 4 (x_hi: 2, x_lo: 2; x = x_hi * 2 + x_lo), y: 4, z: 8, core: 2. Of those that a mesh axis runs over, the one named last changes fastest.
Arguments:
- left_table: float32 [131072, 400], P('dom'), may hold values from -3 to 3
- left_state: float32 [131072], P('dom'), may hold values from 0.01 to 1
- right_table: float32 [131072, 400], P('dom'), may hold values from -30 to 30
- right_state: float32 [131072], P('dom'), may hold values from 0.01 to 1
- rel_table: float32 [3072, 400], P(('dom', 'rep')), may hold values from -3 to 3
- rel_state: float32 [3072], P(('dom', 'rep')), may hold values from 0.01 to 1
- sources: int32 [1048576], P(('dom', 'rep')), may hold values from 0 to 1023
- relations: int32 [1048576], P(('dom', 'rep')), may hold values from 0 to 3071
- targets: int32 [1048576], P(('dom', 'rep')), may hold values from 0 to 1023
- bucket_counts: int32 [128], P('dom'), may hold values from 1 to 6144, as said below
- negatives: int32 [2048, 1024], P(('dom', 'rep')), may hold values from 0 to 1023
Outputs:
- left_next: float32 [131072, 400], P('dom')
- left_state_next: float32 [131072], P('dom')
- right_next: float32 [131072, 400], P('dom')
- right_state_next: float32 [131072], P('dom')
- rel_next: float32 [3072, 400], P(('dom', 'rep'))
- rel_state_next: float32 [3072], P(('dom', 'rep'))
Inputs may be any that keep to these rules, and one draw needn't show every extreme that they name: The live edges of bucket d are its first bucket_counts[d] slots; one bucket has exactly 6144 live edges and another exactly 1.
All inputs are finite; a program needn't handle non-finite values.
Results may differ from a plain program's by a relative error of at most 0.004.
The roundings to bfloat16 on the way count: a program that leaves them out, or rounds other values in their place, can miss the bound.
Values sent between devices are 32-bit elements; how exact they have to be, the bound alone decides.
A program may use at most 128 MiB of HBM per device.

v0:
```python
import jax
import jax.numpy as jnp
from jax import lax
from jax.sharding import PartitionSpec as P

LEARNING_RATE = 0.3


def shifted(block, axis, distance):
    devices = range(lax.axis_size(axis))
    route = [((i - distance) % len(devices), i) for i in devices]
    return lax.ppermute(block, axis, route)


def complex_product(first, second, conjugate):
    half = first.shape[-1] // 2
    first_re = first[..., :half]
    first_im = first[..., half:]
    second_re = second[..., :half]
    second_im = second[..., half:]
    if conjugate:
        second_im = -second_im
    return jnp.concatenate(
        [first_re * second_re - first_im * second_im, first_re * second_im + first_im * second_re],
        axis=-1,
    )


def adagrad(table, state, grad):
    new_state = state + jnp.mean(grad * grad, axis=-1)
    return (table - LEARNING_RATE * grad / jnp.sqrt(new_state)[:, None], new_state)


def group_terms(left_part, right_part, rel_full, src, rel, dst, neg, live):
    heads = left_part[src]
    rel_rows = rel_full[rel]
    tails = right_part[dst]
    query = complex_product(heads, rel_rows, False)
    positive = jnp.sum(query * tails, axis=-1)
    query_low = query.astype(jnp.bfloat16)
    negative_rows = right_part[neg].astype(jnp.bfloat16)
    scores = lax.dot_general(
        query_low, negative_rows, (((1,), (1,)), ((), ())), preferred_element_type=jnp.float32
    )
    top = jnp.maximum(positive, jnp.max(scores, axis=1))
    pos_exp = jnp.exp(positive - top)
    neg_exp = jnp.exp(scores - top[:, None])
    total = pos_exp + jnp.sum(neg_exp, axis=1)
    weight = live / total
    pos_coef = pos_exp * weight - live
    neg_prob = (neg_exp * weight[:, None]).astype(jnp.bfloat16)
    d_query = pos_coef[:, None] * tails + jnp.dot(
        neg_prob, negative_rows, preferred_element_type=jnp.float32
    )
    d_negatives = lax.dot_general(
        neg_prob, query_low, (((0,), (0,)), ((), ())), preferred_element_type=jnp.float32
    )
    d_heads = complex_product(d_query, rel_rows, True)
    d_rel = complex_product(d_query, heads, True)
    d_tails = pos_coef[:, None] * query
    return (d_heads, d_rel, d_tails, d_negatives)


def add_group(grads, left_part, right_part, rel_full, src, rel, dst, neg, live):
    left_grad, right_grad, rel_grad = grads
    d_heads, d_rel, d_tails, d_negatives = group_terms(
        left_part, right_part, rel_full, src, rel, dst, neg, live
    )
    left_grad = left_grad.at[src].add(d_heads)
    right_grad = right_grad.at[dst].add(d_tails).at[neg].add(d_negatives)
    rel_grad = rel_grad.at[rel].add(d_rel)
    return (left_grad, right_grad, rel_grad)


def shards(
    left_table,
    left_state,
    right_table,
    right_state,
    rel_table,
    rel_state,
    sources,
    relations,
    targets,
    bucket_counts,
    negatives,
):
    rel_full = lax.all_gather(rel_table, ("dom", "rep"), axis=0, tiled=True)
    replica = lax.axis_index("rep")
    count = bucket_counts[0]
    blocks = negatives.shape[0]
    width = sources.shape[0] // blocks
    src_c = sources.reshape(blocks, width)
    rel_c = relations.reshape(blocks, width)
    dst_c = targets.reshape(blocks, width)
    order = jnp.arange(blocks, dtype=jnp.int32)
    first = replica * blocks + order
    slots = jnp.arange(width, dtype=jnp.int32)
    live_blocks = jnp.sum((first * width < count).astype(jnp.int32))

    def step(index, grads):
        live = (first[index] * width + slots < count).astype(jnp.float32)
        return add_group(
            grads,
            left_table,
            right_table,
            rel_full,
            src_c[index],
            rel_c[index],
            dst_c[index],
            negatives[index],
            live,
        )

    start = (jnp.zeros_like(left_table), jnp.zeros_like(right_table), jnp.zeros_like(rel_full))
    left_grad, right_grad, rel_grad = lax.fori_loop(0, live_blocks, step, start)
    left_sum, right_sum = lax.psum((left_grad, right_grad), "rep")
    left_next, left_state_next = adagrad(left_table, left_state, left_sum)
    right_new, right_state_new = adagrad(right_table, right_state, right_sum)
    right_next, right_state_next = shifted((right_new, right_state_new), "dom", 1)
    rel_rows = rel_table.shape[0]
    rel_total = lax.psum(rel_grad, ("dom", "rep"))
    rel_mine = lax.dynamic_slice_in_dim(
        rel_total, lax.axis_index(("dom", "rep")) * rel_rows, rel_rows, 0
    )
    rel_next, rel_state_next = adagrad(rel_table, rel_state, rel_mine)
    return (left_next, left_state_next, right_next, right_state_next, rel_next, rel_state_next)


def solution(mesh):
    return jax.shard_map(
        shards,
        mesh=mesh,
        in_specs=(
            P("dom", None),
            P("dom"),
            P("dom", None),
            P("dom"),
            P(("dom", "rep"), None),
            P(("dom", "rep")),
            P(("dom", "rep")),
            P(("dom", "rep")),
            P(("dom", "rep")),
            P("dom"),
            P(("dom", "rep"), None),
        ),
        out_specs=(
            P("dom", None),
            P("dom"),
            P("dom", None),
            P("dom"),
            P(("dom", "rep"), None),
            P(("dom", "rep")),
        ),
        check_vma=False,
    )
```

profile of v0, /device:TPU:2, one launch (start us, length us, event | category | flops | bytes accessed | tf_op | source)
XLA Modules:
  0.0 1848.2 jit_solution(9741729288399243082)
XLA Ops:
  7.2 0.7 all-gather.3.cloned.1.call-update
  8.6 0.7 reshape.168
  9.3 0.7 reshape.169
  10.1 0.7 reshape.170
  10.8 2.8 copy.51
  13.6 1.8 copy.52
  15.4 0.6 fusion.14
  16.0 712.0 %all-gather.3.cloned.1.call-done = f32[256,12,400]{2,1,0:T(8,128)} async-done(((f32[1,12,400]{2,1,0:T(8,128)}), f32[256,12,400]{2,1,0:T(8,128)}) %all-gather.3.cloned.1.call-update) | async-done | bytes 4915216 | tf_op jit(solution)/shard_map/all_gather | solution.py:88
  728.0 8.6 reshape.236
  736.8 1.6 broadcast.106
  738.5 3.4 broadcast_in_dim.2
  741.9 0.8 while.15
  742.7 2.7 copy.53
  745.5 1.7 copy.54
  747.2 0.7 all-reduce.4.cloned.1.call-update
  747.9 795.4 %all-reduce.6.cloned.1.call-done = (f32[1024,400]{0,1:T(8,128)}, f32[1024,400]{0,1:T(8,128)}) async-done(((f32[1024,400]{0,1:T(8,128)}, f32[1024,400]{0,1:T(8,128)}), (f32[1024,400]{0,1:T(8,128)}, f32[1024,400]{0,1:T(8,128)})) %all-reduce.6.cloned.1.call-update) | async-done | bytes 3276816 | tf_op jit(solution)/shard_map/psum | solution.py:117
  1543.3 1.6 multiply_reduce_fusion.1
  1545.0 3.1 divide_subtract_fusion
  1548.1 278.5 %all-reduce.4.cloned.1.call-done = f32[3072,400]{1,0:T(8,128)} async-done(((f32[3072,400]{1,0:T(8,128)}), f32[3072,400]{1,0:T(8,128)}) %all-reduce.4.cloned.1.call-update) | async-done | bytes 4915216 | tf_op jit(solution)/shard_map/psum | solution.py:122
  1826.6 0.9 multiply_reduce_fusion.3
  1828.0 1.5 divide_subtract_fusion.2
  1830.3 1.5 divide_subtract_fusion.1
  1831.8 6.5 collective-permute-done.1
  1838.3 2.8 copy.98
  (29 shorter events, 2.3 us)
Async XLA Ops:
  7.2 6.4 copy-start.5
  7.2 720.9 %all-gather.3.cloned.1.call-start = ((), (), s32[]{:S(2)}) async-start(), calls=%async_computation.1 | async-start | bytes 8421376 | tf_op jit(solution)/shard_map/all_gather | solution.py:88
  7.9 1535.4 %all-reduce.6.cloned.1.call-start = ((), (), s32[]{:S(2)}) async-start(), calls=%async_computation.2 | async-start | bytes 6553600 | tf_op jit(solution)/shard_map/psum | solution.py:117
  747.1 1079.4 %all-reduce.4.cloned.1.call-start = ((), (), s32[]{:S(2)}) async-start(), calls=%async_computation | async-start | bytes 12582912 | tf_op jit(solution)/shard_map/psum | solution.py:122
  747.2 797.7 %copy-start.23 = (f32[1024]{0:T(1024)S(1)}, f32[1024]{0:T(1024)}, u32[]{:S(2)}) copy-start(f32[1024]{0:T(1024)} %param.16) | copy-start | bytes 12292
  747.9 797.1 %copy-start.6 = (f32[1024,400]{0,1:T(8,128)S(1)}, f32[1024,400]{0,1:T(8,128)}, u32[]{:S(2)}) copy-start(f32[1024,400]{0,1:T(8,128)} %param.15) | copy-start | bytes 4915204
  1544.9 282.5 %copy-start.25 = (f32[12]{0:T(128)S(1)}, f32[12]{0:T(128)}, u32[]{:S(2)}) copy-start(f32[12]{0:T(128)} %param.18) | copy-start | bytes 148
  1545.0 283.0 %copy-start.16 = (f32[12,400]{1,0:T(8,128)S(1)}, f32[12,400]{1,0:T(8,128)}, u32[]{:S(2)}) copy-start(f32[12,400]{1,0:T(8,128)} %param.17) | copy-start | bytes 57604
  1545.0 284.5 %copy-start.8 = (f32[1024,400]{0,1:T(8,128)S(1)}, f32[1024,400]{0,1:T(8,128)}, u32[]{:S(2)}) copy-start(f32[1024,400]{0,1:T(8,128)} %get-tuple-element.190) | copy-start | bytes 4915204
  1545.0 284.7 %copy-start.24 = (f32[1024]{0:T(1024)S(1)}, f32[1024]{0:T(1024)}, u32[]{:S(2)}) copy-start(f32[1024]{0:T(1024)} %param.14) | copy-start | bytes 12292
  1548.1 282.2 %copy-start.7 = (f32[1024,400]{0,1:T(8,128)S(1)}, f32[1024,400]{0,1:T(8,128)}, u32[]{:S(2)}) copy-start(f32[1024,400]{0,1:T(8,128)} %param.13) | copy-start | bytes 4915204
  1548.1 290.2 %collective-permute-start = (f32[1024,400]{0,1:T(8,128)}, f32[1024,400]{0,1:T(8,128)}, u32[]{:S(2)}, u32[]{:S(2)}) collective-permute-start(f32[1024,400]{0,1:T(8,128)} %divide_subtract_fusion), channel_id=1, source_target_pairs={{254,0},{0,2},{2,4},{4,6},{6,8},{8,10},{10,12},{12,14},{14,16},{16... | collective-permute-start | bytes 4915208 | tf_op jit(solution)/shard_map/ppermute | solution.py:12
  1829.5 8.8 collective-permute-start.1
Sparse Core Ops, SparseCore 0:
  9.9 718.0 all-gather.2
  747.3 796.0 all-reduce.5
  1549.7 276.8 all-reduce.3
where the time goes:
time: 1860 us; the launch traced here: 1850 us
  waiting for transfers between devices  1790 us (96%)
  local copies, waits for them, and re-layouts  28.5 us (2%)
    psum x1, waiting for transfers between devices, shards(): left_sum, right_sum = lax.psum((left_grad, right_grad), 'rep')  795 us
    all_gather x1, waiting for transfers between devices, shards(): rel_full = lax.all_gather(rel_table, ('dom', 'rep'), axis=0, tiled=True)  712 us
    psum x1, waiting for transfers between devices, shards(): rel_total = lax.psum(rel_grad, ('dom', 'rep'))  278 us
  transfers between devices with their start and end apart: 5, of which 4 were waited for; matrix products, arithmetic and copies ran while one was open for 1% of the time, Pallas kernels for 0%

commit v1 on v0

v1 whole, which is shorter than its diff:
```python
import jax
import jax.numpy as jnp
from jax import lax
from jax.experimental import pallas as pl
from jax.experimental.pallas import tpu as pltpu
from jax.sharding import PartitionSpec as P

RATE = 0.3
D, LANES = 400, 128
E_PART, GROUP, NEG = 1024, 512, 1024
CHUNK = 128
Y, Z, X = 4, 8, 4
SHARD = 48
MAJOR = 32
SLOTS = 4096
F32, BF16, I32 = jnp.float32, jnp.bfloat16, jnp.int32
MESH = pl.DeviceIdType.MESH
VMEM = pl.BlockSpec(memory_space=pltpu.VMEM)
SMEM = pl.BlockSpec(memory_space=pltpu.SMEM)
HBM = pl.BlockSpec(memory_space=pltpu.HBM)
LIMIT = 60 * 2**20


def tiles_of(ref, first, n):
    rows = pl.ds(first, n)
    lane = lax.broadcasted_iota(I32, (n, LANES), 1)
    a, b, c = (ref[rows, pl.ds(j * LANES, LANES)] for j in range(3))
    d = jnp.concatenate([ref[rows, pl.ds(384, 16)], jnp.zeros((n, LANES - 16), F32)], axis=1)
    b1, c1, d1 = (pltpu.roll(v, 56, 1) for v in (b, c, d))
    zero = jnp.zeros((n, LANES), F32)
    return (
        a,
        jnp.where(lane < 72, b, zero),
        jnp.where(lane < 56, b1, c1),
        jnp.where(lane < 56, c1, jnp.where(lane < 72, d1, zero)),
    )


def natural_of(tiles):
    a, b, c, d = tiles
    lane = lax.broadcasted_iota(I32, a.shape, 1)
    c1, d1 = (pltpu.roll(v, 72, 1) for v in (c, d))
    return (a, jnp.where(lane < 72, b, c1), jnp.where(lane < 72, c1, d1), d1[:, :16])


def place():
    dom, xl = lax.axis_index("dom"), lax.axis_index("rep")
    core = lax.rem(dom, 2)
    xh = lax.rem(dom // 2, 2)
    z = lax.rem(dom // 4, Z)
    y = dom // (4 * Z)
    return y, z, xh, core, xl


def device(y, z, xh, core, xl):
    return {"dom": ((y * Z + z) * 2 + xh) * 2 + core, "rep": xl}


def shift_x(xh, xl, k):
    x = lax.rem(xh * 2 + xl + k, X)
    return x // 2, lax.rem(x, 2)


def greet(peers):
    barrier = pltpu.get_barrier_semaphore()
    for peer in peers:
        pl.semaphore_signal(barrier, inc=1, device_id=peer, device_id_type=MESH)
    pl.semaphore_wait(barrier, len(peers))


def neighbours():
    y, z, xh, core, xl = place()
    sib = device(y, z, xh, 1 - core, xl)
    xs = [(*shift_x(xh, xl, k),) for k in range(1, X)]
    xdev = [device(y, z, a, core, b) for a, b in xs]
    ydev = [device(lax.rem(y + k, Y), z, xh, core, xl) for k in range(1, Y)]
    zdev = [device(y, lax.rem(z + k, Z), xh, core, xl) for k in range(1, Z)]
    return sib, xdev, ydev, zdev


def remote(src, dst, send, recv, to):
    copy = pltpu.make_async_remote_copy(
        src_ref=src, dst_ref=dst, send_sem=send, recv_sem=recv, device_id=to, device_id_type=MESH
    )
    copy.start()
    return copy


def family():
    y, z, xh, core, xl = place()
    dom = lax.axis_index("dom")
    twin = dom + 1 - 2 * core
    return {"dom": twin, "rep": xl}, {"dom": dom, "rep": 1 - xl}, {"dom": twin, "rep": 1 - xl}


def prepared(src, dst, send, recv, to):
    return pltpu.make_async_remote_copy(
        src_ref=src, dst_ref=dst, send_sem=send, recv_sem=recv, device_id=to, device_id_type=MESH
    )


def gather_kernel(
    shard, src, rel, dst, neg, count, left, right,
    full, src_all, rel_all, dst_all, neg_all, count_use, left_use, right_use,
    rows, count_rows, zs, zr, ps, pr, cs, cr, es, ea, eb, ts, tr, local,
):
    y, z, xh, core, xl = place()
    sib, xdev, ydev, zdev = neighbours()
    _, partner, diagonal = family()
    greet([sib, partner, diagonal] + xdev + ydev + zdev)
    lane = lax.broadcasted_iota(I32, (12, LANES), 1)
    for j, tile in enumerate(tiles_of(shard, 0, 12)):
        rows[pl.ds(j, 12, stride=4), :] = tile
    first = [remote(rows, full.at[y, z, xh, core, xl], zs.at[k], zr.at[k], zdev[k]) for k in range(Z - 1)]
    own = pltpu.make_async_copy(rows, full.at[y, z, xh, core, xl], local.at[0])
    own.start()
    count_rows[...] = jnp.full((8, LANES), count[0], I32)

    lists = [
        (v, w.at[pl.ds(xl * n, n)])
        for v, w, n in ((src, src_all, SLOTS), (rel, rel_all, SLOTS), (dst, dst_all, SLOTS), (neg, neg_all, 8))
    ]
    twin = {"dom": sib["dom"], "rep": core}
    same = {"dom": lax.axis_index("dom"), "rep": core}
    cross = [prepared(v, w, es.at[i], eb.at[i, xl], twin) for i, (v, w) in enumerate(lists)]
    straight = [prepared(v, w, es.at[4 + i], ea.at[i], same) for i, (v, w) in enumerate(lists)]
    stay = [pltpu.make_async_copy(v, w, local.at[1 + i]) for i, (v, w) in enumerate(lists)]
    things = ((count_rows, count_use), (left, left_use), (right, right_use))
    tables = [prepared(v, w, ts.at[i], tr.at[i], sib) for i, (v, w) in enumerate(things)]
    stay += [pltpu.make_async_copy(v, w, local.at[5 + i]) for i, (v, w) in enumerate(things)]
    for copy in cross:
        copy.start()

    @pl.when(core == xl)
    def _():
        for copy in tables + stay:
            copy.start()

    @pl.when(core != xl)
    def _():
        for copy in straight:
            copy.start()

    own.wait()
    for copy in first:
        copy.wait()
    halves = [pl.ds(0, SHARD // 2), pl.ds(SHARD // 2, SHARD // 2)]
    down = []

    def below(ref):
        i = len(down)
        down.append(remote(ref, ref, cs.at[i], cr.at[i], sib))

    below(full.at[y, :, xh, core, xl])
    second = []
    for half, devs in enumerate((ydev, xdev)):
        part = full.at[y, :, xh, core, xl, halves[half]]
        for k in range(3):
            i = half * 3 + k
            second.append(remote(part, part, ps.at[i], pr.at[i], devs[k]))
    for i, copy in enumerate(second):
        copy.wait()
    third = []
    for half, devs in enumerate((xdev, ydev)):
        part = full.at[:, :, xh, core, xl, halves[0]] if half == 0 else full.at[y, :, :, core, :, halves[1]]
        for k in range(3):
            i = 6 + half * 3 + k
            third.append(remote(part, part, ps.at[i], pr.at[i], devs[k]))
    for k in range(1, 4):
        below(full.at[lax.rem(y + 4 - k, Y), :, xh, core, xl, halves[0]])
        a, b = shift_x(xh, xl, X - k)
        below(full.at[y, :, a, core, b, halves[1]])
    for k in range(1, 4):
        third[k - 1].wait()
        a, b = shift_x(xh, xl, X - k)
        below(full.at[:, :, a, core, b, halves[0]])
        third[2 + k].wait()
        below(full.at[lax.rem(y + 4 - k, Y), :, :, core, :, halves[1]])
    for copy in down:
        copy.wait()
    for copy in cross:
        copy.wait_send()

    @pl.when(core == xl)
    def _():
        for copy in tables:
            copy.wait_send()
        for copy in straight:
            copy.wait_recv()
        for copy in stay:
            copy.wait()

    @pl.when(core != xl)
    def _():
        for copy in tables:
            copy.wait_recv()
        for copy in straight:
            copy.wait_send()
        for i, (v, w) in enumerate(lists):
            for sender in range(2):
                prepared(v, w, es.at[i], eb.at[i, sender], twin).wait_recv()


def gather(shard, src, rel, dst, neg, count, left, right):
    dma = lambda *n: pltpu.SemaphoreType.DMA(n)
    shape = jax.ShapeDtypeStruct
    return pl.pallas_call(
        gather_kernel,
        out_shape=(
            shape((Y, Z, 2, 2, 2, SHARD, LANES), F32),
            shape((2 * SLOTS,), I32), shape((2 * SLOTS,), I32), shape((2 * SLOTS,), I32),
            shape((16, NEG), I32), shape((8, LANES), I32),
            shape((D, E_PART), F32), shape((D, E_PART), F32),
        ),
        in_specs=[VMEM] + [HBM] * 4 + [SMEM] + [HBM] * 2,
        out_specs=(HBM,) * 8,
        scratch_shapes=[
            pltpu.VMEM((SHARD, LANES), F32), pltpu.VMEM((8, LANES), I32),
            dma(7), dma(7), dma(12), dma(12), dma(13), dma(13),
            dma(8), dma(4), dma(4, 2), dma(3), dma(3), dma(8),
        ],
        compiler_params=pltpu.CompilerParams(collective_id=0, has_side_effects=True, vmem_limit_bytes=LIMIT),
        name="gather_relations",
    )(shard, src, rel, dst, neg, count, left, right)


def product(a, b, conjugate):
    if conjugate:
        re = lambda i, j: a[i] * b[i] + a[j] * b[j]
        im = lambda i, j: a[j] * b[i] - a[i] * b[j]
    else:
        re = lambda i, j: a[i] * b[i] - a[j] * b[j]
        im = lambda i, j: a[i] * b[j] + a[j] * b[i]
    return (re(0, 2), re(1, 3), im(0, 2), im(1, 3))


def embedding_tiles(ref, g):
    at = pl.ds(pl.multiple_of(g * LANES, LANES), LANES)
    zero = jnp.zeros((56, LANES), F32)
    full = lambda i: ref[pl.ds(i, LANES), at]
    part = lambda i: jnp.concatenate([ref[pl.ds(i, 72), at], zero], axis=0)
    return full(0), part(128), full(200), part(328)


def compute_kernel(
    parity, counted, src, rel, dst, neg, left_hbm, right_hbm, rels_hbm,
    left_hbm_grad, right_hbm_grad, rel_hbm_grad,
    left, right, rels, left_turned, right_turned, left_grad, right_grad, rel_grad,
    left_rows, right_rows, right_low, low_turned, heads, relat, tails, q_low, prob, neg_t, sems,
):
    count, core = counted[0, 0], parity[0]
    n_blocks = (((count + GROUP - 1) >> 9) + 1 - core) >> 1
    loads = [
        pltpu.make_async_copy(v, w, sems.at[i])
        for i, (v, w) in enumerate(((left_hbm, left), (right_hbm, right), (rels_hbm, rels)))
    ]
    for copy in loads:
        copy.start()
    left_grad[...] = jnp.zeros_like(left_grad)
    right_grad[...] = jnp.zeros_like(right_grad)
    rel_grad[...] = jnp.zeros_like(rel_grad)
    neg_t[...] = jnp.zeros_like(neg_t)
    loads[0].wait()
    loads[1].wait()

    def prepare(g, _):
        first = pl.multiple_of(g * LANES, LANES)
        for j, tile in enumerate(embedding_tiles(left, g)):
            left_rows[pl.ds(4 * first + j, LANES, stride=4), :] = tile.T
        for j, tile in enumerate(embedding_tiles(right, g)):
            low_turned[pl.ds(j * LANES, LANES), pl.ds(first, LANES)] = tile.astype(BF16)
            tile = tile.T
            right_rows[pl.ds(4 * first + j, LANES, stride=4), :] = tile
            right_low[pl.ds(first, LANES), pl.ds(j * LANES, LANES)] = tile.astype(BF16)
        return 0

    lax.fori_loop(0, E_PART // LANES, prepare, 0)
    loads[2].wait()
    unroll = 16

    def block(i, _):
        b = 2 * i + core

        def edges(i):
            at = b * GROUP + i * unroll
            for u in range(unroll):
                yield i * unroll + u, [
                    pl.ds(pl.multiple_of(4 * ids[at + u], 4), 4) for ids in (src, rel, dst)
                ]

        def fetch(i, _):
            for e, (s, r, t) in edges(i):
                to = pl.ds(pl.multiple_of(4 * e, 4), 4)
                heads[to, :] = left_rows[s, :]
                relat[to, :] = rels[r, :]
                tails[to, :] = right_rows[t, :]
            return 0

        lax.fori_loop(0, GROUP // unroll, fetch, 0)

        named = neg[pl.ds(b, 1), :]
        high = (lax.broadcasted_iota(I32, (16, NEG), 0) == (named >> 7)).astype(F32).astype(BF16)
        low = (lax.broadcasted_iota(I32, (LANES, NEG), 0) == (named & 127)).astype(F32).astype(BF16)
        table = lax.dot_general(high, low, (((1,), (1,)), ((), ())), preferred_element_type=F32)
        counts = jnp.concatenate([table[h : h + 1, :] for h in range(E_PART // LANES)], axis=1)
        bias = jnp.where(counts > 0, 0.0, -jnp.inf)

        for ch in range(GROUP // CHUNK):
            rows = pl.ds(ch * CHUNK, CHUNK)
            at = [pl.ds(4 * ch * CHUNK + j, CHUNK, stride=4) for j in range(4)]
            h = [heads[a, :] for a in at]
            r = [relat[a, :] for a in at]
            t = [tails[a, :] for a in at]
            q = product(h, r, False)
            positive = jnp.sum(q[0] * t[0] + q[1] * t[1] + q[2] * t[2] + q[3] * t[3], axis=1, keepdims=True)
            ql = jnp.concatenate([x.astype(BF16) for x in q], axis=1)
            q_low[rows, :] = ql
            scores = jnp.dot(ql, low_turned[...], preferred_element_type=F32) + bias
            slot = b * GROUP + ch * CHUNK + lax.broadcasted_iota(I32, (CHUNK, 1), 0)
            live = (slot < count).astype(F32)
            top = jnp.maximum(positive, jnp.max(scores, axis=1, keepdims=True))
            pos_exp = jnp.exp(positive - top)
            neg_exp = jnp.exp(scores - top)
            total = pos_exp + jnp.sum(neg_exp * counts, axis=1, keepdims=True)
            weight = live / total
            pos_coef = pos_exp * weight - live
            p = (neg_exp * weight).astype(BF16)
            prob[rows, :] = p
            many = p.astype(F32) * counts
            many_high = many.astype(BF16)
            many_low = (many - many_high.astype(F32)).astype(BF16)
            d = jnp.dot(many_high, right_low[...], preferred_element_type=F32) + jnp.dot(
                many_low, right_low[...], preferred_element_type=F32
            )
            dq = [d[:, j * LANES : (j + 1) * LANES] + pos_coef * t[j] for j in range(4)]
            for a, x, y, z in zip(at, product(dq, r, True), product(dq, h, True), q):
                heads[a, :] = x
                relat[a, :] = y
                tails[a, :] = pos_coef * z

        neg_t[...] += counts * lax.dot_general(
            q_low[...], prob[...], (((0,), (0,)), ((), ())), preferred_element_type=F32
        )

        def scatter(i, _):
            for e, (s, r, t) in edges(i):
                of = pl.ds(pl.multiple_of(4 * e, 4), 4)
                for to, grads, terms in ((s, left_grad, heads), (r, rel_grad, relat), (t, right_grad, tails)):
                    grads[to, :] += terms[of, :]
            return 0

        lax.fori_loop(0, GROUP // unroll, scatter, 0)
        return 0

    lax.fori_loop(0, n_blocks, block, 0)
    rel_out = pltpu.make_async_copy(rel_grad, rel_hbm_grad, sems.at[2])
    rel_out.start()

    def finish(g, _):
        first = pl.multiple_of(g * LANES, LANES)
        to = pl.ds(first, LANES)
        for j, (start, size) in enumerate(((0, 128), (128, 72), (200, 128), (328, 72))):
            at = pl.ds(4 * first + j, LANES, stride=4)
            left_turned[pl.ds(start, size), to] = left_grad[at, :].T[:size]
            right_turned[pl.ds(start, size), to] = (
                right_grad[at, :].T[:size] + neg_t[pl.ds(j * LANES, size), to]
            )
        return 0

    lax.fori_loop(0, E_PART // LANES, finish, 0)
    outs = [
        pltpu.make_async_copy(left_turned, left_hbm_grad, sems.at[0]),
        pltpu.make_async_copy(right_turned, right_hbm_grad, sems.at[1]),
    ]
    for copy in outs:
        copy.start()
    for copy in outs:
        copy.wait()
    rel_out.wait()


def compute(parity, counted, src, rel, dst, neg, left, right, rels):
    shape = jax.ShapeDtypeStruct
    n = rels.shape[0]
    table = pltpu.VMEM((D, E_PART), F32)
    rows = pltpu.VMEM((4 * E_PART, LANES), F32)
    block = pltpu.VMEM((4 * GROUP, LANES), F32)
    return pl.pallas_call(
        compute_kernel,
        out_shape=(shape((D, E_PART), F32), shape((D, E_PART), F32), shape((n, LANES), F32)),
        in_specs=[SMEM] * 5 + [VMEM] + [HBM] * 3,
        out_specs=(HBM,) * 3,
        scratch_shapes=[
            table, table, pltpu.VMEM((n, LANES), F32), table, table, rows, rows, pltpu.VMEM((n, LANES), F32),
            rows, rows,
            pltpu.VMEM((E_PART, 512), BF16), pltpu.VMEM((512, E_PART), BF16),
            block, block, block,
            pltpu.VMEM((GROUP, 512), BF16), pltpu.VMEM((GROUP, E_PART), BF16), pltpu.VMEM((512, E_PART), F32),
            pltpu.SemaphoreType.DMA((3,)),
        ],
        compiler_params=pltpu.CompilerParams(vmem_limit_bytes=LIMIT),
        cost_estimate=pl.CostEstimate(flops=20 * 10**9, bytes_accessed=10**8, transcendentals=10**6),
        name="blocks",
    )(parity, counted, src, rel, dst, neg, left, right, rels)


def exchange_kernel(
    left_grad, right_grad, rel_grad,
    left_sum, right_sum, rel_mine,
    left_own, left_sib, right_own, right_sib, acc, from_core, big0, big1, small0, small1, from_x,
    ls, lr, ss, sr, cs, cr, ps, pr, zs, zr, xs, xr, local,
):
    y, z, xh, core, xl = place()
    sib, xdev, ydev, zdev = neighbours()
    _, partner, diagonal = family()
    dom = lax.axis_index("dom")
    n_dom = 4 * Y * Z
    pair = dom - core
    barrier = pltpu.get_barrier_semaphore()
    peers = [sib, partner, diagonal] + xdev + ydev + zdev
    for peer in peers:
        pl.semaphore_signal(barrier, inc=1, device_id=peer, device_id_type=MESH)

    @pl.when(core == 0)
    def _():
        for k in (2, 1):
            behind = {"dom": lax.rem(dom + n_dom - k, n_dom), "rep": 1}
            pl.semaphore_signal(barrier, inc=1, device_id=behind, device_id_type=MESH)

    pl.semaphore_wait(barrier, len(peers) + 2 * xl)

    half = D // 2
    mine, other = pl.ds(core * half, half), pl.ds((1 - core) * half, half)
    pairs = []
    for i, (grad, own, recv) in enumerate(((left_grad, left_own, left_sib), (right_grad, right_own, right_sib))):
        keep = pltpu.make_async_copy(grad.at[mine], own, local.at[i])
        keep.start()
        pairs.append((remote(grad.at[other], recv, ss.at[i], sr.at[i], sib), keep))
    down = remote(rel_grad.at[:, :, :, 1 - core], from_core, cs, cr, sib)
    keep_rel = pltpu.make_async_copy(rel_grad.at[:, :, :, core], acc, local.at[2])
    keep_rel.start()

    left_to = pair + xl
    right_to = lax.rem(pair + xl + 1, n_dom)
    sends, stays = [], []
    for i, (own, recv, out, to) in enumerate(
        ((left_own, left_sib, left_sum, left_to), (right_own, right_sib, right_sum, right_to))
    ):
        for copy in pairs[i]:
            copy.wait()

        def add(j, _):
            at = pl.ds(pl.multiple_of(8 * j, 8), 8)
            own[at, :] += recv[at, :]
            return 0

        lax.fori_loop(0, half // 8, add, 0)
        part = out.at[mine]
        far = prepared(own, part, ls.at[i, 0], lr.at[i, core, 0], {"dom": to, "rep": 1 - xl})
        near = prepared(own, part, ls.at[i, 1], lr.at[i, core, 1], {"dom": to, "rep": xl})
        stay = pltpu.make_async_copy(own, part, local.at[3 + i])
        far.start()
        self_too = to == dom

        @pl.when(self_too)
        def _():
            stay.start()

        @pl.when(jnp.logical_not(self_too))
        def _():
            near.start()

        sends.append((far, near, stay, self_too))

    keep_rel.wait()
    down.wait()

    def add_core(i, _):
        acc[i // Z, lax.rem(i, Z)] += from_core[i // Z, lax.rem(i, Z)]
        return 0

    lax.fori_loop(0, Y * Z, add_core, 0)

    cut = [pl.ds(0, MAJOR), pl.ds(MAJOR, SHARD - MAJOR)]
    one = []
    for k in range(1, Y):
        t = lax.rem(y + k, Y)
        one.append(remote(acc.at[t, :, :, :, cut[0]], big0.at[k - 1], ps.at[k - 1], pr.at[k - 1], ydev[k - 1]))
    for k in range(1, Z):
        t = lax.rem(z + k, Z)
        one.append(remote(acc.at[:, t, :, :, cut[1]], big1.at[k - 1], zs.at[k - 1], zr.at[k - 1], zdev[k - 1]))
    for copy in one:
        copy.wait()

    def add_y(i, _):
        acc[y, i, :, :, cut[0]] += big0[0, i] + big0[1, i] + big0[2, i]
        return 0

    lax.fori_loop(0, Z, add_y, 0)

    def add_z(i, _):
        total = acc[i, z, :, :, cut[1]]
        for k in range(Z - 1):
            total = total + big1[k, i]
        acc[i, z, :, :, cut[1]] = total
        return 0

    lax.fori_loop(0, Y, add_z, 0)
    two = []
    for k in range(1, Z):
        t = lax.rem(z + k, Z)
        two.append(remote(acc.at[y, t, :, :, cut[0]], small0.at[k - 1], zs.at[6 + k], zr.at[6 + k], zdev[k - 1]))
    for k in range(1, Y):
        t = lax.rem(y + k, Y)
        two.append(remote(acc.at[t, z, :, :, cut[1]], small1.at[k - 1], ps.at[2 + k], pr.at[2 + k], ydev[k - 1]))
    for copy in two:
        copy.wait()
    total = acc[y, z, :, :, cut[0]]
    for k in range(Z - 1):
        total = total + small0[k]
    acc[y, z, :, :, cut[0]] = total
    acc[y, z, :, :, cut[1]] += small1[0] + small1[1] + small1[2]
    three = []
    for k in range(1, X):
        a, b = shift_x(xh, xl, k)
        three.append(remote(acc.at[y, z, a, b], from_x.at[k - 1], xs.at[k - 1], xr.at[k - 1], xdev[k - 1]))
    for copy in three:
        copy.wait()
    rel_mine[...] = acc[y, z, xh, xl] + from_x[0] + from_x[1] + from_x[2]

    for far, near, stay, self_too in sends:
        far.wait_send()

        @pl.when(self_too)
        def _():
            stay.wait()

        @pl.when(jnp.logical_not(self_too))
        def _():
            near.wait_send()

    for i, owner in ((0, core), (1, 1 - core)):
        own, out = ((left_own, left_sum), (right_own, right_sum))[i]
        for sender in range(2):
            part = out.at[pl.ds(sender * half, half)]
            local_chip = owner == xl
            to_self = jnp.logical_and(local_chip, jnp.logical_and(sender == core, jnp.logical_or(i == 0, core == 1)))
            came = lambda kind: prepared(own, part, ls.at[i, 0], lr.at[i, sender, kind], sib)

            @pl.when(jnp.logical_not(local_chip))
            def _():
                came(0).wait_recv()

            @pl.when(jnp.logical_and(local_chip, jnp.logical_not(to_self)))
            def _():
                came(1).wait_recv()


def exchange(left_grad, right_grad, rel_grad):
    dma = lambda *n: pltpu.SemaphoreType.DMA(n)
    shape = jax.ShapeDtypeStruct
    table = shape((D, E_PART), F32)
    half = pltpu.VMEM((D // 2, E_PART), F32)
    minor = SHARD - MAJOR
    return pl.pallas_call(
        exchange_kernel,
        out_shape=(table, table, shape((SHARD, LANES), F32)),
        in_specs=[HBM] * 3,
        out_specs=(HBM, HBM, VMEM),
        scratch_shapes=[half] * 4
        + [
            pltpu.VMEM((Y, Z, 2, 2, SHARD, LANES), F32),
            pltpu.VMEM((Y, Z, 2, 2, SHARD, LANES), F32),
            pltpu.VMEM((Y - 1, Z, 2, 2, MAJOR, LANES), F32),
            pltpu.VMEM((Z - 1, Y, 2, 2, minor, LANES), F32),
            pltpu.VMEM((Z - 1, 2, 2, MAJOR, LANES), F32),
            pltpu.VMEM((Y - 1, 2, 2, minor, LANES), F32),
            pltpu.VMEM((X - 1, SHARD, LANES), F32),
            dma(2, 2), dma(2, 2, 2), dma(2), dma(2),
            pltpu.SemaphoreType.DMA, pltpu.SemaphoreType.DMA,
            dma(6), dma(6), dma(14), dma(14), dma(3), dma(3), dma(5),
        ],
        compiler_params=pltpu.CompilerParams(collective_id=1, has_side_effects=True, vmem_limit_bytes=LIMIT),
        name="exchange_gradients",
    )(left_grad, right_grad, rel_grad)


def update_kernel(
    left, left_state, left_sum, right, right_state, right_sum, rel, rel_state, rel_grad,
    left_next, left_state_next, right_next, right_state_next, rel_next, rel_state_next,
):
    for table, state, total, after, state_after in (
        (left, left_state, left_sum, left_next, left_state_next),
        (right, right_state, right_sum, right_next, right_state_next),
    ):
        grad = total[...]
        fresh = state[...] + jnp.sum(grad * grad, axis=0, keepdims=True) * (1.0 / D)
        state_after[...] = fresh
        after[...] = table[...] - grad * (RATE / jnp.sqrt(fresh))

    @pl.when(pl.program_id(0) == 0)
    def _():
        n = rel.shape[0]
        same = lax.broadcasted_iota(I32, (n, n), 0) == lax.broadcasted_iota(I32, (n, n), 1)
        column = lambda row: jnp.sum(jnp.where(same, jnp.broadcast_to(row, (n, n)), 0.0), axis=1, keepdims=True)
        across = lambda col: jnp.sum(jnp.where(same, jnp.broadcast_to(col, (n, n)), 0.0), axis=0, keepdims=True)
        grad = [rel_grad[pl.ds(j, n, stride=4), :] for j in range(4)]
        square = jnp.sum(sum(v * v for v in grad), axis=1, keepdims=True) * (1.0 / D)
        fresh = column(rel_state[...]) + square
        rel_state_next[...] = across(fresh)
        scale = RATE / jnp.sqrt(fresh)
        for j, change in enumerate(natural_of([v * scale for v in grad])):
            cols = pl.ds(j * LANES, change.shape[1])
            rel_next[:, cols] = rel[:, cols] - change


def update(left, left_state, left_sum, right, right_state, right_sum, rel, rel_state, rel_grad):
    wide = 2 * LANES
    table = pl.BlockSpec((D, wide), lambda g: (0, g))
    state = pl.BlockSpec((1, wide), lambda g: (0, g))
    whole = lambda shape: pl.BlockSpec(shape, lambda g: (0, 0))
    shape = jax.ShapeDtypeStruct
    big, row = shape((D, E_PART), F32), shape((1, E_PART), F32)
    return pl.pallas_call(
        update_kernel,
        grid=(E_PART // wide,),
        out_shape=(big, row, big, row, shape(rel.shape, F32), shape(rel_state.shape, F32)),
        in_specs=[table, state, table] * 2 + [whole(rel.shape), whole(rel_state.shape), whole((SHARD, LANES))],
        out_specs=(table, state, table, state, whole(rel.shape), whole(rel_state.shape)),
        compiler_params=pltpu.CompilerParams(vmem_limit_bytes=LIMIT),
        name="adagrad",
    )(left, left_state, left_sum, right, right_state, right_sum, rel, rel_state, rel_grad)


def shards(
    left_table, left_state, right_table, right_state, rel_table, rel_state,
    sources, relations, targets, bucket_counts, negatives,
):
    left, right = left_table.T, right_table.T
    rels, src, rel, dst, neg, counted, left_use, right_use = gather(
        rel_table, sources, relations, targets, negatives, bucket_counts, left, right
    )
    n_dom = 4 * Y * Z
    route = [((i - 1) % n_dom, i) for i in range(n_dom)]
    held, held_state, rels = lax.optimization_barrier((right_table, right_state, rels))
    held = lax.ppermute(held, "dom", route)
    held_state = lax.ppermute(held_state, "dom", route)
    parity = lax.rem(lax.axis_index("dom"), 2).reshape(1)
    left_grad, right_grad, rel_grad = compute(
        parity, counted, src, rel, dst, neg, left_use, right_use, rels.reshape(-1, LANES)
    )
    left_sum, right_sum, rel_mine = exchange(
        left_grad, right_grad, rel_grad.reshape(Y, Z, 2, 2, 2, SHARD, LANES)
    )
    left_next, left_after, right_next, right_after, rel_next, rel_after = update(
        left, left_state[None], left_sum, held.T, held_state[None], right_sum, rel_table, rel_state[None], rel_mine
    )
    return left_next.T, left_after[0], right_next.T, right_after[0], rel_next, rel_after[0]


def solution(mesh):
    both = P(("dom", "rep"))
    rows = P(("dom", "rep"), None)
    table, state = P("dom", None), P("dom")
    return jax.shard_map(
        shards,
        mesh=mesh,
        in_specs=(table, state, table, state, rows, both, both, both, both, state, rows),
        out_specs=(table, state, table, state, rows, both),
        check_vma=False,
    )
```

time: 1860 us -> 271 us (0.15)
  the two profiles are of different devices: /device:TPU:2 before, /device:TPU:24 now
where the time goes in v1:
time: 271 us
  Pallas kernels  265 us (98%)
  starting transfers between devices  3.2 us (1%)
    pallas_call x1, Pallas kernels, gather(): pl.pallas_call(gather_kernel, out_shape=(shape((Y, Z, 2, 2, 2, SHARD, LAN...  112 us
    pallas_call x1, Pallas kernels, exchange(): pl.pallas_call(exchange_kernel, out_shape=(table, table, shape((SHARD, LA...  96.4 us
    pallas_call x1, Pallas kernels, compute(): pl.pallas_call(compute_kernel, out_shape=(shape((D, E_PART), F32), shape(...  50.9 us
    pallas_call x1, Pallas kernels, update(): pl.pallas_call(update_kernel, grid=(E_PART // wide,), out_shape=(big, row...  5.45 us
  transfers between devices with their start and end apart: 2, of which 0 were waited for; matrix products, arithmetic and copies ran while one was open for 0% of the time, Pallas kernels for 54%

profile of v1, /device:TPU:24, one launch (start us, length us, event | category | flops | bytes accessed | tf_op | source)
XLA Modules:
  0.0 270.6 jit_solution(575679592872284759)
XLA Ops:
  1.3 0.0 copy-start.3
  1.3 0.0 copy-start
  1.3 112.1 %gather_relations.1 = (f32[4,8,2,2,2,48,128]{6,5,4,3,2,1,0:T(8,128)}, s32[8192]{0:T(1024)}, s32[8192]{0:T(1024)}, s32[8192]{0:T(1024)}, s32[16,1024]{1,0:T(8,128...) custom-call(f32[12,400]{1,0:T(8,128)} %rel.3, s32[4096]{0:T(1024)} %src.1, s32[4096]{0:T(1024)} %rel.2, ...), custom_call_target="tpu_custom_call" | custom-call | tf_op jit(solution)/shard_map/gather_relations/pallas_call | solution.py:207
  113.4 0.0 copy-done.3
  113.4 0.1 collective-permute-start.1
  113.5 0.0 copy-done
  113.5 3.1 %collective-permute-start = (f32[1024,400]{0,1:T(8,128)S(1)}, f32[1024,400]{0,1:T(8,128)S(1)}, u32[]{:S(2)}, u32[]{:S(2)}) collective-permute-start(f32[1024,400]{0,1:T(8,128)S(1)} %copy-done), channel_id=1, source_target_pairs={{254,0},{0,2},{2,4},{4,6},{6,8},{8,10},{10,12},{12,14},{14,16},{16... | collective-permute-start | bytes 4915208 | tf_op jit(solution)/shard_map/ppermute | solution.py:646
  116.6 50.9 %blocks.1 = (f32[400,1024]{1,0:T(8,128)}, f32[400,1024]{1,0:T(8,128)}, f32[12288,128]{1,0:T(8,128)}) custom-call(s32[1]{0:T(128)} %bitcast.2.parity, s32[8,128]{1,0:T(8,128)} %get-tuple-element.29.counted, s32[8192]{0:T(1024)} %get-tuple-element.30.src, s32[8192]{0:T(1024)} %get-tuple-element.31.rel, s32[8192]{0:T(1024)} %get-tuple-element.32.dst, ...), custom_call_target="tpu_custom_call" | custom-call | flops 20000000000 | bytes 100000000 | tf_op jit(solution)/shard_map/blocks/pallas_call | solution.py:388
  167.5 96.4 %exchange_gradients.1 = (f32[400,1024]{1,0:T(8,128)}, f32[400,1024]{1,0:T(8,128)}, f32[48,128]{1,0:T(8,128)}) custom-call(f32[400,1024]{1,0:T(8,128)} %get-tuple-element.38.left_grad, f32[400,1024]{1,0:T(8,128)} %get-tuple-element.39.right_grad, f32[4,8,2,2,2,48,128]{6,5,4,3,2,1,0:T(8,128)} %bitcast.16), custom_call_target="tpu_custom_call" | custom-call | tf_op jit(solution)/shard_map/exchange_gradients/pallas_call | solution.py:565
  264.0 0.0 collective-permute-done.1
  264.0 0.0 copy-start.2
  264.0 0.0 collective-permute-done
  264.0 0.0 copy-start.1
  264.0 0.6 copy-done.2
  264.6 0.6 copy-done.1
  265.2 5.4 %adagrad.1 = (f32[400,1024]{1,0:T(8,128)}, f32[1,1024]{1,0:T(1,128)}, f32[400,1024]{1,0:T(8,128)}, f32[1,1024]{1,0:T(1,128)}, f32[12,400]{1,0:T(8,128)}, /*index=5*/f32[1,12]{1,0:T(1,128)}) custom-call(f32[400,1024]{1,0:T(8,128)} %bitcast.15, f32[1,1024]{1,0:T(1,128)} %bitcast.19, f32[400,1024]{1,0:T(8,128)} %get-tuple-element.41.left_sum, ...), custom_call_target="tpu_custom_call" | custom-call | tf_op jit(solution)/shard_map/adagrad/pallas_call | solution.py:624
Async XLA Ops:
  1.3 112.1 %copy-start.3 = (f32[1024]{0:T(1024)S(1)}, f32[1024]{0:T(1024)}, u32[]{:S(2)}) copy-start(f32[1024]{0:T(1024)} %param.14) | copy-start | bytes 12292
  1.3 112.2 %copy-start = (f32[1024,400]{0,1:T(8,128)S(1)}, f32[1024,400]{0,1:T(8,128)}, u32[]{:S(2)}) copy-start(f32[1024,400]{0,1:T(8,128)} %param.13) | copy-start | bytes 4915204
  113.4 150.6 %collective-permute-start.1 = (f32[1024]{0:T(1024)S(1)}, f32[1024]{0:T(1024)S(1)}, u32[]{:S(2)}, u32[]{:S(2)}) collective-permute-start(f32[1024]{0:T(1024)S(1)} %copy-done.3), channel_id=1, source_target_pairs={{254,0},{0,2},{2,4},{4,6},{6,8},{8,10},{10,12},{12,14},{14,16},{16... | collective-permute-start | bytes 12296 | tf_op jit(solution)/shard_map/ppermute | solution.py:647
  113.5 150.5 %collective-permute-start = (f32[1024,400]{0,1:T(8,128)S(1)}, f32[1024,400]{0,1:T(8,128)S(1)}, u32[]{:S(2)}, u32[]{:S(2)}) collective-permute-start(f32[1024,400]{0,1:T(8,128)S(1)} %copy-done), channel_id=1, source_target_pairs={{254,0},{0,2},{2,4},{4,6},{6,8},{8,10},{10,12},{12,14},{14,16},{16... | collective-permute-start | bytes 4915208 | tf_op jit(solution)/shard_map/ppermute | solution.py:646
  264.0 0.6 copy-start.2
  264.0 1.2 copy-start.1

commit v2 on v1

--- a/solution.py
+++ b/solution.py
@@ -11,7 +11,6 @@
 CHUNK = 128
 Y, Z, X = 4, 8, 4
 SHARD = 48
-MAJOR = 32
 SLOTS = 4096
 F32, BF16, I32 = jnp.float32, jnp.bfloat16, jnp.int32
 MESH = pl.DeviceIdType.MESH
@@ -108,7 +107,6 @@
     sib, xdev, ydev, zdev = neighbours()
     _, partner, diagonal = family()
     greet([sib, partner, diagonal] + xdev + ydev + zdev)
-    lane = lax.broadcasted_iota(I32, (12, LANES), 1)
     for j, tile in enumerate(tiles_of(shard, 0, 12)):
         rows[pl.ds(j, 12, stride=4), :] = tile
     first = [remote(rows, full.at[y, z, xh, core, xl], zs.at[k], zr.at[k], zdev[k]) for k in range(Z - 1)]
@@ -127,7 +125,7 @@
     stay = [pltpu.make_async_copy(v, w, local.at[1 + i]) for i, (v, w) in enumerate(lists)]
     things = ((count_rows, count_use), (left, left_use), (right, right_use))
     tables = [prepared(v, w, ts.at[i], tr.at[i], sib) for i, (v, w) in enumerate(things)]
-    stay += [pltpu.make_async_copy(v, w, local.at[5 + i]) for i, (v, w) in enumerate(things)]
+    stay.append(pltpu.make_async_copy(count_rows, count_use, local.at[5]))
     for copy in cross:
         copy.start()
 
@@ -217,7 +215,7 @@
         scratch_shapes=[
             pltpu.VMEM((SHARD, LANES), F32), pltpu.VMEM((8, LANES), I32),
             dma(7), dma(7), dma(12), dma(12), dma(13), dma(13),
-            dma(8), dma(4), dma(4, 2), dma(3), dma(3), dma(8),
+            dma(8), dma(4), dma(4, 2), dma(3), dma(3), dma(6),
         ],
         compiler_params=pltpu.CompilerParams(collective_id=0, has_side_effects=True, vmem_limit_bytes=LIMIT),
         name="gather_relations",
@@ -243,19 +241,28 @@
 
 
 def compute_kernel(
-    parity, counted, src, rel, dst, neg, left_hbm, right_hbm, rels_hbm,
+    spot, counted, src, rel, dst, neg, left_here, right_here, left_sent, right_sent, rels_hbm,
     left_hbm_grad, right_hbm_grad, rel_hbm_grad,
     left, right, rels, left_turned, right_turned, left_grad, right_grad, rel_grad,
     left_rows, right_rows, right_low, low_turned, heads, relat, tails, q_low, prob, neg_t, sems,
 ):
-    count, core = counted[0, 0], parity[0]
+    count, core, at_home = counted[0, 0], spot[0], spot[1]
     n_blocks = (((count + GROUP - 1) >> 9) + 1 - core) >> 1
-    loads = [
-        pltpu.make_async_copy(v, w, sems.at[i])
-        for i, (v, w) in enumerate(((left_hbm, left), (right_hbm, right), (rels_hbm, rels)))
-    ]
-    for copy in loads:
-        copy.start()
+    tables = ((left_here, left_sent, left), (right_here, right_sent, right))
+    loads = [pltpu.make_async_copy(v, w, sems.at[i]) for i, (v, _, w) in enumerate(tables)]
+    loads.append(pltpu.make_async_copy(rels_hbm, rels, sems.at[2]))
+
+    @pl.when(at_home == 1)
+    def _():
+        for copy in loads[:2]:
+            copy.start()
+
+    @pl.when(at_home == 0)
+    def _():
+        for i, (_, v, w) in enumerate(tables):
+            pltpu.make_async_copy(v, w, sems.at[i]).start()
+
+    loads[2].start()
     left_grad[...] = jnp.zeros_like(left_grad)
     right_grad[...] = jnp.zeros_like(right_grad)
     rel_grad[...] = jnp.zeros_like(rel_grad)
@@ -379,7 +386,7 @@
     rel_out.wait()
 
 
-def compute(parity, counted, src, rel, dst, neg, left, right, rels):
+def compute(spot, counted, src, rel, dst, neg, left, right, left_sent, right_sent, rels):
     shape = jax.ShapeDtypeStruct
     n = rels.shape[0]
     table = pltpu.VMEM((D, E_PART), F32)
@@ -388,7 +395,7 @@
     return pl.pallas_call(
         compute_kernel,
         out_shape=(shape((D, E_PART), F32), shape((D, E_PART), F32), shape((n, LANES), F32)),
-        in_specs=[SMEM] * 5 + [VMEM] + [HBM] * 3,
+        in_specs=[SMEM] * 5 + [VMEM] + [HBM] * 5,
         out_specs=(HBM,) * 3,
         scratch_shapes=[
             table, table, pltpu.VMEM((n, LANES), F32), table, table, rows, rows, pltpu.VMEM((n, LANES), F32),
@@ -401,14 +408,14 @@
         compiler_params=pltpu.CompilerParams(vmem_limit_bytes=LIMIT),
         cost_estimate=pl.CostEstimate(flops=20 * 10**9, bytes_accessed=10**8, transcendentals=10**6),
         name="blocks",
-    )(parity, counted, src, rel, dst, neg, left, right, rels)
+    )(spot, counted, src, rel, dst, neg, left, right, left_sent, right_sent, rels)
 
 
 def exchange_kernel(
     left_grad, right_grad, rel_grad,
     left_sum, right_sum, rel_mine,
-    left_own, left_sib, right_own, right_sib, acc, from_core, big0, big1, small0, small1, from_x,
-    ls, lr, ss, sr, cs, cr, ps, pr, zs, zr, xs, xr, local,
+    left_own, left_sib, right_own, right_sib, acc, from_core, from_y, from_x, from_z,
+    ls, lr, ss, sr, cs, cr, ys, yr, xs, xr, zs, zr, local,
 ):
     y, z, xh, core, xl = place()
     sib, xdev, ydev, zdev = neighbours()
@@ -436,7 +443,11 @@
         keep = pltpu.make_async_copy(grad.at[mine], own, local.at[i])
         keep.start()
         pairs.append((remote(grad.at[other], recv, ss.at[i], sr.at[i], sib), keep))
-    down = remote(rel_grad.at[:, :, :, 1 - core], from_core, cs, cr, sib)
+    cut = [pl.ds(0, SHARD // 2), pl.ds(SHARD // 2, SHARD // 2)]
+    down = [
+        remote(rel_grad.at[:, :, :, 1 - core, :, c], from_core.at[:, :, :, :, c], cs.at[i], cr.at[i], sib)
+        for i, c in enumerate(cut)
+    ]
     keep_rel = pltpu.make_async_copy(rel_grad.at[:, :, :, core], acc, local.at[2])
     keep_rel.start()
 
@@ -473,60 +484,53 @@
         sends.append((far, near, stay, self_too))
 
     keep_rel.wait()
-    down.wait()
-
-    def add_core(i, _):
-        acc[i // Z, lax.rem(i, Z)] += from_core[i // Z, lax.rem(i, Z)]
-        return 0
-
-    lax.fori_loop(0, Y * Z, add_core, 0)
-
-    cut = [pl.ds(0, MAJOR), pl.ds(MAJOR, SHARD - MAJOR)]
-    one = []
-    for k in range(1, Y):
-        t = lax.rem(y + k, Y)
-        one.append(remote(acc.at[t, :, :, :, cut[0]], big0.at[k - 1], ps.at[k - 1], pr.at[k - 1], ydev[k - 1]))
-    for k in range(1, Z):
-        t = lax.rem(z + k, Z)
-        one.append(remote(acc.at[:, t, :, :, cut[1]], big1.at[k - 1], zs.at[k - 1], zr.at[k - 1], zdev[k - 1]))
-    for copy in one:
-        copy.wait()
-
-    def add_y(i, _):
-        acc[y, i, :, :, cut[0]] += big0[0, i] + big0[1, i] + big0[2, i]
-        return 0
-
-    lax.fori_loop(0, Z, add_y, 0)
-
-    def add_z(i, _):
-        total = acc[i, z, :, :, cut[1]]
+    by_y, by_x, by_z = [], [], []
+    for i, c in enumerate(cut):
+        down[i].wait()
+
+        def add_core(n, _):
+            at = (n // Z, lax.rem(n, Z), slice(None), slice(None), c)
+            acc[at] += from_core[at]
+            return 0
+
+        lax.fori_loop(0, Y * Z, add_core, 0)
+        by_y.append([])
+        for k in range(1, Y):
+            t, n = lax.rem(y + k, Y), 3 * i + k - 1
+            by_y[i].append(remote(acc.at[t, :, :, :, c], from_y.at[n], ys.at[n], yr.at[n], ydev[k - 1]))
+    for i, c in enumerate(cut):
+        for copy in by_y[i]:
+            copy.wait()
+
+        def add_y(n, _):
+            acc[y, n, :, :, c] += from_y[3 * i, n] + from_y[3 * i + 1, n] + from_y[3 * i + 2, n]
+            return 0
+
+        lax.fori_loop(0, Z, add_y, 0)
+        by_x.append([])
+        for k in range(1, X):
+            (a, b), n = shift_x(xh, xl, k), 3 * i + k - 1
+            by_x[i].append(remote(acc.at[y, :, a, b, c], from_x.at[n], xs.at[n], xr.at[n], xdev[k - 1]))
+    for i, c in enumerate(cut):
+        for copy in by_x[i]:
+            copy.wait()
+
+        def add_x(n, _):
+            acc[y, n, xh, xl, c] += from_x[3 * i, n] + from_x[3 * i + 1, n] + from_x[3 * i + 2, n]
+            return 0
+
+        lax.fori_loop(0, Z, add_x, 0)
+        by_z.append([])
+        for k in range(1, Z):
+            t, n = lax.rem(z + k, Z), 7 * i + k - 1
+            by_z[i].append(remote(acc.at[y, t, xh, xl, c], from_z.at[n], zs.at[n], zr.at[n], zdev[k - 1]))
+    for i, c in enumerate(cut):
+        for copy in by_z[i]:
+            copy.wait()
+        total = acc[y, z, xh, xl, c]
         for k in range(Z - 1):
-            total = total + big1[k, i]
-        acc[i, z, :, :, cut[1]] = total
-        return 0
-
-    lax.fori_loop(0, Y, add_z, 0)
-    two = []
-    for k in range(1, Z):
-        t = lax.rem(z + k, Z)
-        two.append(remote(acc.at[y, t, :, :, cut[0]], small0.at[k - 1], zs.at[6 + k], zr.at[6 + k], zdev[k - 1]))
-    for k in range(1, Y):
-        t = lax.rem(y + k, Y)
-        two.append(remote(acc.at[t, z, :, :, cut[1]], small1.at[k - 1], ps.at[2 + k], pr.at[2 + k], ydev[k - 1]))
-    for copy in two:
-        copy.wait()
-    total = acc[y, z, :, :, cut[0]]
-    for k in range(Z - 1):
-        total = total + small0[k]
-    acc[y, z, :, :, cut[0]] = total
-    acc[y, z, :, :, cut[1]] += small1[0] + small1[1] + small1[2]
-    three = []
-    for k in range(1, X):
-        a, b = shift_x(xh, xl, k)
-        three.append(remote(acc.at[y, z, a, b], from_x.at[k - 1], xs.at[k - 1], xr.at[k - 1], xdev[k - 1]))
-    for copy in three:
-        copy.wait()
-    rel_mine[...] = acc[y, z, xh, xl] + from_x[0] + from_x[1] + from_x[2]
+            total = total + from_z[7 * i + k]
+        rel_mine[c, :] = total
 
     for far, near, stay, self_too in sends:
         far.wait_send()
@@ -561,7 +565,6 @@
     shape = jax.ShapeDtypeStruct
     table = shape((D, E_PART), F32)
     half = pltpu.VMEM((D // 2, E_PART), F32)
-    minor = SHARD - MAJOR
     return pl.pallas_call(
         exchange_kernel,
         out_shape=(table, table, shape((SHARD, LANES), F32)),
@@ -571,14 +574,11 @@
         + [
             pltpu.VMEM((Y, Z, 2, 2, SHARD, LANES), F32),
             pltpu.VMEM((Y, Z, 2, 2, SHARD, LANES), F32),
-            pltpu.VMEM((Y - 1, Z, 2, 2, MAJOR, LANES), F32),
-            pltpu.VMEM((Z - 1, Y, 2, 2, minor, LANES), F32),
-            pltpu.VMEM((Z - 1, 2, 2, MAJOR, LANES), F32),
-            pltpu.VMEM((Y - 1, 2, 2, minor, LANES), F32),
-            pltpu.VMEM((X - 1, SHARD, LANES), F32),
+            pltpu.VMEM((6, Z, 2, 2, SHARD // 2, LANES), F32),
+            pltpu.VMEM((6, Z, SHARD // 2, LANES), F32),
+            pltpu.VMEM((14, SHARD // 2, LANES), F32),
             dma(2, 2), dma(2, 2, 2), dma(2), dma(2),
-            pltpu.SemaphoreType.DMA, pltpu.SemaphoreType.DMA,
-            dma(6), dma(6), dma(14), dma(14), dma(3), dma(3), dma(5),
+            dma(2), dma(2), dma(6), dma(6), dma(6), dma(6), dma(14), dma(14), dma(5),
         ],
         compiler_params=pltpu.CompilerParams(collective_id=1, has_side_effects=True, vmem_limit_bytes=LIMIT),
         name="exchange_gradients",
@@ -645,9 +645,10 @@
     held, held_state, rels = lax.optimization_barrier((right_table, right_state, rels))
     held = lax.ppermute(held, "dom", route)
     held_state = lax.ppermute(held_state, "dom", route)
-    parity = lax.rem(lax.axis_index("dom"), 2).reshape(1)
+    core = lax.rem(lax.axis_index("dom"), 2)
+    spot = jnp.stack([core, (core == lax.axis_index("rep")).astype(I32)])
     left_grad, right_grad, rel_grad = compute(
-        parity, counted, src, rel, dst, neg, left_use, right_use, rels.reshape(-1, LANES)
+        spot, counted, src, rel, dst, neg, left, right, left_use, right_use, rels.reshape(-1, LANES)
     )
     left_sum, right_sum, rel_mine = exchange(
         left_grad, right_grad, rel_grad.reshape(Y, Z, 2, 2, 2, SHARD, LANES)

time: 271 us -> 186 us (0.69)
  the two profiles are of different devices: /device:TPU:24 before, /device:TPU:2 now
where the time goes in v2:
time: 186 us; the launch traced here: 183 us
  Pallas kernels  179 us (96%)
    pallas_call x1, Pallas kernels, exchange(): pl.pallas_call(exchange_kernel, out_shape=(table, table, shape((SHARD, LA...  78.6 us
    pallas_call x1, Pallas kernels, compute(): pl.pallas_call(compute_kernel, out_shape=(shape((D, E_PART), F32), shape(...  50.9 us
    pallas_call x1, Pallas kernels, gather(): pl.pallas_call(gather_kernel, out_shape=(shape((Y, Z, 2, 2, 2, SHARD, LAN...  43.5 us
    pallas_call x1, Pallas kernels, update(): pl.pallas_call(update_kernel, grid=(E_PART // wide,), out_shape=(big, row...  5.45 us
  transfers between devices with their start and end apart: 2, of which 0 were waited for; matrix products, arithmetic and copies ran while one was open for 0% of the time, Pallas kernels for 71%

profile of v2, /device:TPU:2, one launch (start us, length us, event | category | flops | bytes accessed | tf_op | source)
XLA Modules:
  0.0 183.1 jit_solution(16817371631088711610)
XLA Ops:
  1.3 0.0 copy-start.3
  1.3 0.0 copy-start
  1.3 43.5 %gather_relations.1 = (f32[4,8,2,2,2,48,128]{6,5,4,3,2,1,0:T(8,128)}, s32[8192]{0:T(1024)}, s32[8192]{0:T(1024)}, s32[8192]{0:T(1024)}, s32[16,1024]{1,0:T(8,128...) custom-call(f32[12,400]{1,0:T(8,128)} %rel.3, s32[4096]{0:T(1024)} %src.1, s32[4096]{0:T(1024)} %rel.2, ...), custom_call_target="tpu_custom_call" | custom-call | tf_op jit(solution)/shard_map/gather_relations/pallas_call | solution.py:205
  44.8 0.0 copy-done.3
  44.8 0.5 collective-permute-start.1
  45.3 0.0 copy-done
  45.3 1.0 collective-permute-start
  46.3 0.6 pad_add_fusion.spot
  46.8 50.9 %blocks.1 = (f32[400,1024]{1,0:T(8,128)}, f32[400,1024]{1,0:T(8,128)}, f32[12288,128]{1,0:T(8,128)}) custom-call(s32[2]{0:T(128)} %pad_add_fusion.spot, s32[8,128]{1,0:T(8,128)} %get-tuple-element.29.counted, s32[8192]{0:T(1024)} %get-tuple-element.30.src, s32[8192]{0:T(1024)} %get-tuple-element.31.rel, s32[8192]{0:T(1024)} %get-tuple-element.32.dst, ...), custom_call_target="tpu_custom_call" | custom-call | flops 20000000000 | bytes 100000000 | tf_op jit(solution)/shard_map/blocks/pallas_call | solution.py:395
  97.8 78.6 %exchange_gradients.1 = (f32[400,1024]{1,0:T(8,128)}, f32[400,1024]{1,0:T(8,128)}, f32[48,128]{1,0:T(8,128)}) custom-call(f32[400,1024]{1,0:T(8,128)} %get-tuple-element.38.left_grad, f32[400,1024]{1,0:T(8,128)} %get-tuple-element.39.right_grad, f32[4,8,2,2,2,48,128]{6,5,4,3,2,1,0:T(8,128)} %bitcast.18), custom_call_target="tpu_custom_call" | custom-call | tf_op jit(solution)/shard_map/exchange_gradients/pallas_call | solution.py:568
  176.4 0.0 collective-permute-done.1
  176.4 0.0 copy-start.2
  176.5 0.0 collective-permute-done
  176.5 0.0 copy-start.1
  176.5 0.6 copy-done.2
  177.0 0.6 copy-done.1
  177.6 5.4 %adagrad.1 = (f32[400,1024]{1,0:T(8,128)}, f32[1,1024]{1,0:T(1,128)}, f32[400,1024]{1,0:T(8,128)}, f32[1,1024]{1,0:T(1,128)}, f32[12,400]{1,0:T(8,128)}, /*index=5*/f32[1,12]{1,0:T(1,128)}) custom-call(f32[400,1024]{1,0:T(8,128)} %bitcast.17, f32[1,1024]{1,0:T(1,128)} %bitcast.22, f32[400,1024]{1,0:T(8,128)} %get-tuple-element.41.left_sum, ...), custom_call_target="tpu_custom_call" | custom-call | tf_op jit(solution)/shard_map/adagrad/pallas_call | solution.py:624
Async XLA Ops:
  1.3 43.5 %copy-start.3 = (f32[1024]{0:T(1024)S(1)}, f32[1024]{0:T(1024)}, u32[]{:S(2)}) copy-start(f32[1024]{0:T(1024)} %param.14) | copy-start | bytes 12292
  1.3 44.0 %copy-start = (f32[1024,400]{0,1:T(8,128)S(1)}, f32[1024,400]{0,1:T(8,128)}, u32[]{:S(2)}) copy-start(f32[1024,400]{0,1:T(8,128)} %param.13) | copy-start | bytes 4915204
  44.8 131.6 %collective-permute-start.1 = (f32[1024]{0:T(1024)S(1)}, f32[1024]{0:T(1024)S(1)}, u32[]{:S(2)}, u32[]{:S(2)}) collective-permute-start(f32[1024]{0:T(1024)S(1)} %copy-done.3), channel_id=1, source_target_pairs={{254,0},{0,2},{2,4},{4,6},{6,8},{8,10},{10,12},{12,14},{14,16},{16... | collective-permute-start | bytes 12296 | tf_op jit(solution)/shard_map/ppermute | solution.py:647
  45.3 131.2 %collective-permute-start = (f32[1024,400]{0,1:T(8,128)S(1)}, f32[1024,400]{0,1:T(8,128)S(1)}, u32[]{:S(2)}, u32[]{:S(2)}) collective-permute-start(f32[1024,400]{0,1:T(8,128)S(1)} %copy-done), channel_id=1, source_target_pairs={{254,0},{0,2},{2,4},{4,6},{6,8},{8,10},{10,12},{12,14},{14,16},{16... | collective-permute-start | bytes 4915208 | tf_op jit(solution)/shard_map/ppermute | solution.py:646
  176.4 0.6 copy-start.2
  176.5 1.2 copy-start.1

commit v3 on v2

--- a/solution.py
+++ b/solution.py
@@ -8,7 +8,7 @@
 RATE = 0.3
 D, LANES = 400, 128
 E_PART, GROUP, NEG = 1024, 512, 1024
-CHUNK = 128
+CHUNK = 512
 Y, Z, X = 4, 8, 4
 SHARD = 48
 SLOTS = 4096
@@ -241,10 +241,10 @@
 
 
 def compute_kernel(
-    spot, counted, src, rel, dst, neg, left_here, right_here, left_sent, right_sent, rels_hbm,
+    spot, counted, src_hbm, rel_hbm, dst_hbm, neg, left_here, right_here, left_sent, right_sent, rels_hbm,
     left_hbm_grad, right_hbm_grad, rel_hbm_grad,
     left, right, rels, left_turned, right_turned, left_grad, right_grad, rel_grad,
-    left_rows, right_rows, right_low, low_turned, heads, relat, tails, q_low, prob, neg_t, sems,
+    left_rows, right_rows, right_low, low_turned, heads, relat, tails, q_low, prob, neg_t, src, rel, dst, ids_in, sems, id_sems,
 ):
     count, core, at_home = counted[0, 0], spot[0], spot[1]
     n_blocks = (((count + GROUP - 1) >> 9) + 1 - core) >> 1
@@ -263,6 +263,15 @@
             pltpu.make_async_copy(v, w, sems.at[i]).start()
 
     loads[2].start()
+    scaled = []
+    for i, (v, w) in enumerate(((src_hbm, src), (rel_hbm, rel), (dst_hbm, dst))):
+        held = ids_in.at[pl.ds(2 * SLOTS * i, 2 * SLOTS)]
+        scaled.append((held, pltpu.make_async_copy(v, held, id_sems.at[i]), pltpu.make_async_copy(held, w, id_sems.at[i])))
+        scaled[i][1].start()
+    for held, came, goes in scaled:
+        came.wait()
+        held[...] = held[...] * 4
+        goes.start()
     left_grad[...] = jnp.zeros_like(left_grad)
     right_grad[...] = jnp.zeros_like(right_grad)
     rel_grad[...] = jnp.zeros_like(rel_grad)
@@ -283,27 +292,32 @@
 
     lax.fori_loop(0, E_PART // LANES, prepare, 0)
     loads[2].wait()
-    unroll = 16
+    unroll = 32
+
+    def rows_of(b, e):
+        return [pl.ds(pl.multiple_of(ids[b * GROUP + e], 4), 4) for ids in (src, rel, dst)]
+
+    def fetch(b, slot, e):
+        s, r, t = rows_of(b, e)
+        to = pl.ds(pl.multiple_of(slot + 4 * e, 4), 4)
+        heads[to, :] = left_rows[s, :]
+        relat[to, :] = rels[r, :]
+        tails[to, :] = right_rows[t, :]
+
+    for _, _, goes in scaled:
+        goes.wait()
+
+    def first_fetch(n, _):
+        for u in range(unroll):
+            fetch(core, 0, n * unroll + u)
+        return 0
+
+    lax.fori_loop(0, GROUP // unroll, first_fetch, 0)
 
     def block(i, _):
         b = 2 * i + core
-
-        def edges(i):
-            at = b * GROUP + i * unroll
-            for u in range(unroll):
-                yield i * unroll + u, [
-                    pl.ds(pl.multiple_of(4 * ids[at + u], 4), 4) for ids in (src, rel, dst)
-                ]
-
-        def fetch(i, _):
-            for e, (s, r, t) in edges(i):
-                to = pl.ds(pl.multiple_of(4 * e, 4), 4)
-                heads[to, :] = left_rows[s, :]
-                relat[to, :] = rels[r, :]
-                tails[to, :] = right_rows[t, :]
-            return 0
-
-        lax.fori_loop(0, GROUP // unroll, fetch, 0)
+        slot = pl.multiple_of(lax.rem(i, 2) * 4 * GROUP, 4 * GROUP)
+        after = pl.multiple_of(4 * GROUP - slot, 4 * GROUP)
 
         named = neg[pl.ds(b, 1), :]
         high = (lax.broadcasted_iota(I32, (16, NEG), 0) == (named >> 7)).astype(F32).astype(BF16)
@@ -314,7 +328,7 @@
 
         for ch in range(GROUP // CHUNK):
             rows = pl.ds(ch * CHUNK, CHUNK)
-            at = [pl.ds(4 * ch * CHUNK + j, CHUNK, stride=4) for j in range(4)]
+            at = [pl.ds(slot + 4 * ch * CHUNK + j, CHUNK, stride=4) for j in range(4)]
             h = [heads[a, :] for a in at]
             r = [relat[a, :] for a in at]
             t = [tails[a, :] for a in at]
@@ -323,8 +337,8 @@
             ql = jnp.concatenate([x.astype(BF16) for x in q], axis=1)
             q_low[rows, :] = ql
             scores = jnp.dot(ql, low_turned[...], preferred_element_type=F32) + bias
-            slot = b * GROUP + ch * CHUNK + lax.broadcasted_iota(I32, (CHUNK, 1), 0)
-            live = (slot < count).astype(F32)
+            place_in = b * GROUP + ch * CHUNK + lax.broadcasted_iota(I32, (CHUNK, 1), 0)
+            live = (place_in < count).astype(F32)
             top = jnp.maximum(positive, jnp.max(scores, axis=1, keepdims=True))
             pos_exp = jnp.exp(positive - top)
             neg_exp = jnp.exp(scores - top)
@@ -349,11 +363,13 @@
             q_low[...], prob[...], (((0,), (0,)), ((), ())), preferred_element_type=F32
         )
 
-        def scatter(i, _):
-            for e, (s, r, t) in edges(i):
-                of = pl.ds(pl.multiple_of(4 * e, 4), 4)
-                for to, grads, terms in ((s, left_grad, heads), (r, rel_grad, relat), (t, right_grad, tails)):
-                    grads[to, :] += terms[of, :]
+        def scatter(n, _):
+            for u in range(unroll):
+                e = n * unroll + u
+                of = pl.ds(pl.multiple_of(slot + 4 * e, 4), 4)
+                for to, total, terms in zip(rows_of(b, e), (left_grad, rel_grad, right_grad), (heads, relat, tails)):
+                    total[to, :] += terms[of, :]
+                fetch(b + 2, after, e)
             return 0
 
         lax.fori_loop(0, GROUP // unroll, scatter, 0)
@@ -391,11 +407,11 @@
     n = rels.shape[0]
     table = pltpu.VMEM((D, E_PART), F32)
     rows = pltpu.VMEM((4 * E_PART, LANES), F32)
-    block = pltpu.VMEM((4 * GROUP, LANES), F32)
+    block = pltpu.VMEM((8 * GROUP, LANES), F32)
     return pl.pallas_call(
         compute_kernel,
         out_shape=(shape((D, E_PART), F32), shape((D, E_PART), F32), shape((n, LANES), F32)),
-        in_specs=[SMEM] * 5 + [VMEM] + [HBM] * 5,
+        in_specs=[SMEM] * 2 + [HBM] * 3 + [VMEM] + [HBM] * 5,
         out_specs=(HBM,) * 3,
         scratch_shapes=[
             table, table, pltpu.VMEM((n, LANES), F32), table, table, rows, rows, pltpu.VMEM((n, LANES), F32),
@@ -403,7 +419,9 @@
             pltpu.VMEM((E_PART, 512), BF16), pltpu.VMEM((512, E_PART), BF16),
             block, block, block,
             pltpu.VMEM((GROUP, 512), BF16), pltpu.VMEM((GROUP, E_PART), BF16), pltpu.VMEM((512, E_PART), F32),
-            pltpu.SemaphoreType.DMA((3,)),
+            pltpu.SMEM((2 * SLOTS,), I32), pltpu.SMEM((2 * SLOTS,), I32), pltpu.SMEM((2 * SLOTS,), I32),
+            pltpu.VMEM((6 * SLOTS,), I32),
+            pltpu.SemaphoreType.DMA((3,)), pltpu.SemaphoreType.DMA((3,)),
         ],
         compiler_params=pltpu.CompilerParams(vmem_limit_bytes=LIMIT),
         cost_estimate=pl.CostEstimate(flops=20 * 10**9, bytes_accessed=10**8, transcendentals=10**6),
@@ -414,7 +432,8 @@
 def exchange_kernel(
     left_grad, right_grad, rel_grad,
     left_sum, right_sum, rel_mine,
-    left_own, left_sib, right_own, right_sib, acc, from_core, from_y, from_x, from_z,
+    left_own, left_sib, right_own, right_sib, acc, from_core,
+    from_y0, from_y2, from_x0, from_x2, from_z0, from_z2, low_z, low_y, low_x,
     ls, lr, ss, sr, cs, cr, ys, yr, xs, xr, zs, zr, local,
 ):
     y, z, xh, core, xl = place()
@@ -443,7 +462,7 @@
         keep = pltpu.make_async_copy(grad.at[mine], own, local.at[i])
         keep.start()
         pairs.append((remote(grad.at[other], recv, ss.at[i], sr.at[i], sib), keep))
-    cut = [pl.ds(0, SHARD // 2), pl.ds(SHARD // 2, SHARD // 2)]
+    cut = [pl.ds(0, 24), pl.ds(24, 8), pl.ds(32, 16)]
     down = [
         remote(rel_grad.at[:, :, :, 1 - core, :, c], from_core.at[:, :, :, :, c], cs.at[i], cr.at[i], sib)
         for i, c in enumerate(cut)
@@ -484,7 +503,10 @@
         sends.append((far, near, stay, self_too))
 
     keep_rel.wait()
-    by_y, by_x, by_z = [], [], []
+    by_y, by_x, by_z = {}, {}, {}
+    wide = (from_y0, None, from_y2)
+    middle = (from_x0, None, from_x2)
+    last = (from_z0, None, from_z2)
     for i, c in enumerate(cut):
         down[i].wait()
 
@@ -494,43 +516,79 @@
             return 0
 
         lax.fori_loop(0, Y * Z, add_core, 0)
-        by_y.append([])
+        if i == 1:
+            by_z[i] = [
+                remote(acc.at[:, lax.rem(z + k, Z), :, :, c], low_z.at[k - 1], zs.at[6 + k], zr.at[6 + k], zdev[k - 1])
+                for k in range(1, Z)
+            ]
+            continue
+        by_y[i] = []
         for k in range(1, Y):
             t, n = lax.rem(y + k, Y), 3 * i + k - 1
-            by_y[i].append(remote(acc.at[t, :, :, :, c], from_y.at[n], ys.at[n], yr.at[n], ydev[k - 1]))
-    for i, c in enumerate(cut):
+            by_y[i].append(remote(acc.at[t, :, :, :, c], wide[i].at[k - 1], ys.at[n], yr.at[n], ydev[k - 1]))
+    for i in (0, 2):
+        c, came = cut[i], wide[i]
         for copy in by_y[i]:
             copy.wait()
 
         def add_y(n, _):
-            acc[y, n, :, :, c] += from_y[3 * i, n] + from_y[3 * i + 1, n] + from_y[3 * i + 2, n]
+            acc[y, n, :, :, c] += came[0, n] + came[1, n] + came[2, n]
             return 0
 
         lax.fori_loop(0, Z, add_y, 0)
-        by_x.append([])
+        by_x[i] = []
         for k in range(1, X):
             (a, b), n = shift_x(xh, xl, k), 3 * i + k - 1
-            by_x[i].append(remote(acc.at[y, :, a, b, c], from_x.at[n], xs.at[n], xr.at[n], xdev[k - 1]))
-    for i, c in enumerate(cut):
+            by_x[i].append(remote(acc.at[y, :, a, b, c], middle[i].at[k - 1], xs.at[n], xr.at[n], xdev[k - 1]))
+    c = cut[1]
+    for copy in by_z[1]:
+        copy.wait()
+
+    def add_z(n, _):
+        total = acc[n, z, :, :, c]
+        for k in range(Z - 1):
+            total = total + low_z[k, n]
+        acc[n, z, :, :, c] = total
+        return 0
+
+    lax.fori_loop(0, Y, add_z, 0)
+    by_y[1] = [
+        remote(acc.at[lax.rem(y + k, Y), z, :, :, c], low_y.at[k - 1], ys.at[2 + k], yr.at[2 + k], ydev[k - 1])
+        for k in range(1, Y)
+    ]
+    for i in (0, 2):
+        c, came = cut[i], middle[i]
         for copy in by_x[i]:
             copy.wait()
 
         def add_x(n, _):
-            acc[y, n, xh, xl, c] += from_x[3 * i, n] + from_x[3 * i + 1, n] + from_x[3 * i + 2, n]
+            acc[y, n, xh, xl, c] += came[0, n] + came[1, n] + came[2, n]
             return 0
 
         lax.fori_loop(0, Z, add_x, 0)
-        by_z.append([])
+        by_z[i] = []
         for k in range(1, Z):
             t, n = lax.rem(z + k, Z), 7 * i + k - 1
-            by_z[i].append(remote(acc.at[y, t, xh, xl, c], from_z.at[n], zs.at[n], zr.at[n], zdev[k - 1]))
-    for i, c in enumerate(cut):
+            by_z[i].append(remote(acc.at[y, t, xh, xl, c], last[i].at[k - 1], zs.at[n], zr.at[n], zdev[k - 1]))
+    c = cut[1]
+    for copy in by_y[1]:
+        copy.wait()
+    acc[y, z, :, :, c] += low_y[0] + low_y[1] + low_y[2]
+    by_x[1] = []
+    for k in range(1, X):
+        a, b = shift_x(xh, xl, k)
+        by_x[1].append(remote(acc.at[y, z, a, b, c], low_x.at[k - 1], xs.at[2 + k], xr.at[2 + k], xdev[k - 1]))
+    for i in (0, 2):
+        c = cut[i]
         for copy in by_z[i]:
             copy.wait()
         total = acc[y, z, xh, xl, c]
         for k in range(Z - 1):
-            total = total + from_z[7 * i + k]
+            total = total + last[i][k]
         rel_mine[c, :] = total
+    for copy in by_x[1]:
+        copy.wait()
+    rel_mine[cut[1], :] = acc[y, z, xh, xl, cut[1]] + low_x[0] + low_x[1] + low_x[2]
 
     for far, near, stay, self_too in sends:
         far.wait_send()
@@ -574,11 +632,12 @@
         + [
             pltpu.VMEM((Y, Z, 2, 2, SHARD, LANES), F32),
             pltpu.VMEM((Y, Z, 2, 2, SHARD, LANES), F32),
-            pltpu.VMEM((6, Z, 2, 2, SHARD // 2, LANES), F32),
-            pltpu.VMEM((6, Z, SHARD // 2, LANES), F32),
-            pltpu.VMEM((14, SHARD // 2, LANES), F32),
+            pltpu.VMEM((3, Z, 2, 2, 24, LANES), F32), pltpu.VMEM((3, Z, 2, 2, 16, LANES), F32),
+            pltpu.VMEM((3, Z, 24, LANES), F32), pltpu.VMEM((3, Z, 16, LANES), F32),
+            pltpu.VMEM((7, 24, LANES), F32), pltpu.VMEM((7, 16, LANES), F32),
+            pltpu.VMEM((7, Y, 2, 2, 8, LANES), F32), pltpu.VMEM((3, 2, 2, 8, LANES), F32), pltpu.VMEM((3, 8, LANES), F32),
             dma(2, 2), dma(2, 2, 2), dma(2), dma(2),
-            dma(2), dma(2), dma(6), dma(6), dma(6), dma(6), dma(14), dma(14), dma(5),
+            dma(3), dma(3), dma(9), dma(9), dma(9), dma(9), dma(21), dma(21), dma(5),
         ],
         compiler_params=pltpu.CompilerParams(collective_id=1, has_side_effects=True, vmem_limit_bytes=LIMIT),
         name="exchange_gradients",

time: 186 us -> 168 us (0.903); the launches traced: 183 us -> 168 us
  Pallas kernels: 179 us -> 163 us
    pallas_call x1, Pallas kernels: 50.9 us -> 36.2 us  [compute(): pl.pallas_call(compute_kernel, out_shape=(shape((D, E_PART), F32), shape(...]
  transfers between devices with their start and end apart: 2 -> 2, of which waited for: 0 -> 0; matrix products, arithmetic and copies ran while one was open for 0% -> 0% of each run, Pallas kernels for 71% -> 68%
where the time goes in v3:
time: 168 us
  Pallas kernels  163 us (97%)
    pallas_call x1, Pallas kernels, exchange(): pl.pallas_call(exchange_kernel, out_shape=(table, table, shape((SHARD, LA...  77.9 us
    pallas_call x1, Pallas kernels, gather(): pl.pallas_call(gather_kernel, out_shape=(shape((Y, Z, 2, 2, 2, SHARD, LAN...  43.5 us
    pallas_call x1, Pallas kernels, compute(): pl.pallas_call(compute_kernel, out_shape=(shape((D, E_PART), F32), shape(...  36.2 us
    pallas_call x1, Pallas kernels, update(): pl.pallas_call(update_kernel, grid=(E_PART // wide,), out_shape=(big, row...  5.45 us
  transfers between devices with their start and end apart: 2, of which 0 were waited for; matrix products, arithmetic and copies ran while one was open for 0% of the time, Pallas kernels for 68%

profile of v3, /device:TPU:2, one launch (start us, length us, event | category | flops | bytes accessed | tf_op | source)
XLA Modules:
  0.0 167.6 jit_solution(2032978737393789438)
XLA Ops:
  1.3 0.0 copy-start.3
  1.3 0.0 copy-start
  1.3 43.5 %gather_relations.1 = (f32[4,8,2,2,2,48,128]{6,5,4,3,2,1,0:T(8,128)}, s32[8192]{0:T(1024)}, s32[8192]{0:T(1024)}, s32[8192]{0:T(1024)}, s32[16,1024]{1,0:T(8,128...) custom-call(f32[12,400]{1,0:T(8,128)} %rel.3, s32[4096]{0:T(1024)} %src.1, s32[4096]{0:T(1024)} %rel.2, ...), custom_call_target="tpu_custom_call" | custom-call | tf_op jit(solution)/shard_map/gather_relations/pallas_call | solution.py:205
  44.8 0.0 copy-done.3
  44.8 0.5 collective-permute-start.1
  45.3 0.0 copy-done
  45.3 1.0 collective-permute-start
  46.3 0.6 pad_add_fusion.spot
  46.8 36.2 %blocks.1 = (f32[400,1024]{1,0:T(8,128)}, f32[400,1024]{1,0:T(8,128)}, f32[12288,128]{1,0:T(8,128)}) custom-call(s32[2]{0:T(128)} %pad_add_fusion.spot, s32[8,128]{1,0:T(8,128)} %get-tuple-element.29.counted, s32[8192]{0:T(1024)} %get-tuple-element.30.src_hbm, s32[8192]{0:T(1024)} %get-tuple-element.31.rel_hbm, s32[8192]{0:T(1024)} %get-tuple-element.32.dst_hbm, ...), custom_call_target="tpu_custom_call" | custom-call | flops 20000000000 | bytes 100000000 | tf_op jit(solution)/shard_map/blocks/pallas_call | solution.py:411
  83.0 77.9 %exchange_gradients.1 = (f32[400,1024]{1,0:T(8,128)}, f32[400,1024]{1,0:T(8,128)}, f32[48,128]{1,0:T(8,128)}) custom-call(f32[400,1024]{1,0:T(8,128)} %get-tuple-element.38.left_grad, f32[400,1024]{1,0:T(8,128)} %get-tuple-element.39.right_grad, f32[4,8,2,2,2,48,128]{6,5,4,3,2,1,0:T(8,128)} %bitcast.18), custom_call_target="tpu_custom_call" | custom-call | tf_op jit(solution)/shard_map/exchange_gradients/pallas_call | solution.py:626
  161.0 0.0 collective-permute-done.1
  161.0 0.0 copy-start.2
  161.0 0.0 collective-permute-done
  161.0 0.0 copy-start.1
  161.0 0.6 copy-done.2
  161.6 0.6 copy-done.1
  162.2 5.4 %adagrad.1 = (f32[400,1024]{1,0:T(8,128)}, f32[1,1024]{1,0:T(1,128)}, f32[400,1024]{1,0:T(8,128)}, f32[1,1024]{1,0:T(1,128)}, f32[12,400]{1,0:T(8,128)}, /*index=5*/f32[1,12]{1,0:T(1,128)}) custom-call(f32[400,1024]{1,0:T(8,128)} %bitcast.17, f32[1,1024]{1,0:T(1,128)} %bitcast.22, f32[400,1024]{1,0:T(8,128)} %get-tuple-element.41.left_sum, ...), custom_call_target="tpu_custom_call" | custom-call | tf_op jit(solution)/shard_map/adagrad/pallas_call | solution.py:683
Async XLA Ops:
  1.3 43.5 %copy-start.3 = (f32[1024]{0:T(1024)S(1)}, f32[1024]{0:T(1024)}, u32[]{:S(2)}) copy-start(f32[1024]{0:T(1024)} %param.14) | copy-start | bytes 12292
  1.3 44.0 %copy-start = (f32[1024,400]{0,1:T(8,128)S(1)}, f32[1024,400]{0,1:T(8,128)}, u32[]{:S(2)}) copy-start(f32[1024,400]{0,1:T(8,128)} %param.13) | copy-start | bytes 4915204
  44.8 116.1 %collective-permute-start.1 = (f32[1024]{0:T(1024)S(1)}, f32[1024]{0:T(1024)S(1)}, u32[]{:S(2)}, u32[]{:S(2)}) collective-permute-start(f32[1024]{0:T(1024)S(1)} %copy-done.3), channel_id=1, source_target_pairs={{254,0},{0,2},{2,4},{4,6},{6,8},{8,10},{10,12},{12,14},{14,16},{16... | collective-permute-start | bytes 12296 | tf_op jit(solution)/shard_map/ppermute | solution.py:706
  45.3 115.7 %collective-permute-start = (f32[1024,400]{0,1:T(8,128)S(1)}, f32[1024,400]{0,1:T(8,128)S(1)}, u32[]{:S(2)}, u32[]{:S(2)}) collective-permute-start(f32[1024,400]{0,1:T(8,128)S(1)} %copy-done), channel_id=1, source_target_pairs={{254,0},{0,2},{2,4},{4,6},{6,8},{8,10},{10,12},{12,14},{14,16},{16... | collective-permute-start | bytes 4915208 | tf_op jit(solution)/shard_map/ppermute | solution.py:705
  161.0 0.6 copy-start.2
  161.0 1.2 copy-start.1

commit v4 on v3

--- a/solution.py
+++ b/solution.py
@@ -100,7 +100,7 @@
 
 def gather_kernel(
     shard, src, rel, dst, neg, count, left, right,
-    full, src_all, rel_all, dst_all, neg_all, count_use, left_use, right_use,
+    full, src_all, rel_all, dst_all, neg_all, count_use, spot, left_use, right_use,
     rows, count_rows, zs, zr, ps, pr, cs, cr, es, ea, eb, ts, tr, local,
 ):
     y, z, xh, core, xl = place()
@@ -113,6 +113,8 @@
     own = pltpu.make_async_copy(rows, full.at[y, z, xh, core, xl], local.at[0])
     own.start()
     count_rows[...] = jnp.full((8, LANES), count[0], I32)
+    line = lax.broadcasted_iota(I32, (8, LANES), 0)
+    spot[...] = jnp.where(line == 0, core, jnp.where(core == xl, 1, 0))
 
     lists = [
         (v, w.at[pl.ds(xl * n, n)])
@@ -158,22 +160,46 @@
             second.append(remote(part, part, ps.at[i], pr.at[i], devs[k]))
     for i, copy in enumerate(second):
         copy.wait()
-    third = []
-    for half, devs in enumerate((xdev, ydev)):
-        part = full.at[:, :, xh, core, xl, halves[0]] if half == 0 else full.at[y, :, :, core, :, halves[1]]
-        for k in range(3):
-            i = 6 + half * 3 + k
-            third.append(remote(part, part, ps.at[i], pr.at[i], devs[k]))
+    low, high = 0, 1
+
+    def part(half, k, which):
+        if half == 0:
+            a, b = shift_x(xh, xl, k)
+            return full.at[pl.ds(2 * which, 2), :, a, core, b, halves[0]]
+        return full.at[lax.rem(y + k, Y), pl.ds(4 * which, 4), :, core, :, halves[1]]
+
+    third = {}
+    ends = ((xdev[0], xdev[2]), (ydev[0], ydev[2]))
+
+    def ring(half, k, which, up):
+        i = 6 + len(third)
+        ref = part(half, k, which)
+        third[half, k, which, up] = remote(ref, ref, ps.at[i], pr.at[i], ends[half][1 - up])
+
+    for up, which in ((1, low), (0, high), (1, high), (0, low)):
+        for half in range(2):
+            ring(half, 0, which, up)
     for k in range(1, 4):
         below(full.at[lax.rem(y + 4 - k, Y), :, xh, core, xl, halves[0]])
         a, b = shift_x(xh, xl, X - k)
         below(full.at[y, :, a, core, b, halves[1]])
-    for k in range(1, 4):
-        third[k - 1].wait()
-        a, b = shift_x(xh, xl, X - k)
-        below(full.at[:, :, a, core, b, halves[0]])
-        third[2 + k].wait()
-        below(full.at[lax.rem(y + 4 - k, Y), :, :, core, :, halves[1]])
+    for half in range(2):
+        third[half, 0, low, 1].wait()
+        ring(half, 3, low, 1)
+        third[half, 0, high, 0].wait()
+        ring(half, 1, high, 0)
+        below(part(half, 3, low))
+        below(part(half, 1, high))
+    for half in range(2):
+        third[half, 0, high, 1].wait()
+        below(part(half, 3, high))
+        third[half, 0, low, 0].wait()
+        below(part(half, 1, low))
+    for half in range(2):
+        third[half, 3, low, 1].wait()
+        below(part(half, 2, low))
+        third[half, 1, high, 0].wait()
+        below(part(half, 2, high))
     for copy in down:
         copy.wait()
     for copy in cross:
@@ -207,14 +233,14 @@
         out_shape=(
             shape((Y, Z, 2, 2, 2, SHARD, LANES), F32),
             shape((2 * SLOTS,), I32), shape((2 * SLOTS,), I32), shape((2 * SLOTS,), I32),
-            shape((16, NEG), I32), shape((8, LANES), I32),
+            shape((16, NEG), I32), shape((8, LANES), I32), shape((8, LANES), I32),
             shape((D, E_PART), F32), shape((D, E_PART), F32),
         ),
         in_specs=[VMEM] + [HBM] * 4 + [SMEM] + [HBM] * 2,
-        out_specs=(HBM,) * 8,
+        out_specs=(HBM,) * 6 + (VMEM,) + (HBM,) * 2,
         scratch_shapes=[
             pltpu.VMEM((SHARD, LANES), F32), pltpu.VMEM((8, LANES), I32),
-            dma(7), dma(7), dma(12), dma(12), dma(13), dma(13),
+            dma(7), dma(7), dma(18), dma(18), dma(19), dma(19),
             dma(8), dma(4), dma(4, 2), dma(3), dma(3), dma(6),
         ],
         compiler_params=pltpu.CompilerParams(collective_id=0, has_side_effects=True, vmem_limit_bytes=LIMIT),
@@ -246,7 +272,7 @@
     left, right, rels, left_turned, right_turned, left_grad, right_grad, rel_grad,
     left_rows, right_rows, right_low, low_turned, heads, relat, tails, q_low, prob, neg_t, src, rel, dst, ids_in, sems, id_sems,
 ):
-    count, core, at_home = counted[0, 0], spot[0], spot[1]
+    count, core, at_home = counted[0, 0], spot[0, 0], spot[1, 0]
     n_blocks = (((count + GROUP - 1) >> 9) + 1 - core) >> 1
     tables = ((left_here, left_sent, left), (right_here, right_sent, right))
     loads = [pltpu.make_async_copy(v, w, sems.at[i]) for i, (v, _, w) in enumerate(tables)]
@@ -433,7 +459,7 @@
     left_grad, right_grad, rel_grad,
     left_sum, right_sum, rel_mine,
     left_own, left_sib, right_own, right_sib, acc, from_core,
-    from_y0, from_y2, from_x0, from_x2, from_z0, from_z2, low_z, low_y, low_x,
+    on_up0, on_down0, came_up0, came_down0, on_up2, on_down2, came_up2, came_down2, from_x0, from_x2, from_z0, from_z2, low_z, low_y, low_x,
     ls, lr, ss, sr, cs, cr, ys, yr, xs, xr, zs, zr, local,
 ):
     y, z, xh, core, xl = place()
@@ -503,8 +529,16 @@
         sends.append((far, near, stay, self_too))
 
     keep_rel.wait()
-    by_y, by_x, by_z = {}, {}, {}
-    wide = (from_y0, None, from_y2)
+    by_y, by_x, by_z = {0: [], 2: []}, {}, {}
+    on_up, on_down = (on_up0, None, on_up2), (on_down0, None, on_down2)
+    came_up, came_down = (came_up0, None, came_up2), (came_down0, None, came_down2)
+    up, far, below = (lax.rem(y + k, Y) for k in range(1, Y))
+    lo, hi = pl.ds(0, 4), pl.ds(4, 4)
+
+    def passing(i, src, dst, to):
+        n = 3 * i + len(by_y[i])
+        by_y[i].append(remote(src, dst, ys.at[n], yr.at[n], to))
+
     middle = (from_x0, None, from_x2)
     last = (from_z0, None, from_z2)
     for i, c in enumerate(cut):
@@ -522,17 +556,35 @@
                 for k in range(1, Z)
             ]
             continue
-        by_y[i] = []
-        for k in range(1, Y):
-            t, n = lax.rem(y + k, Y), 3 * i + k - 1
-            by_y[i].append(remote(acc.at[t, :, :, :, c], wide[i].at[k - 1], ys.at[n], yr.at[n], ydev[k - 1]))
+        passing(i, acc.at[far, lo, :, :, c], on_up[i], ydev[0])
+        passing(i, acc.at[far, hi, :, :, c], on_down[i], ydev[2])
+        passing(i, acc.at[up, hi, :, :, c], came_up[i].at[hi], ydev[0])
+        passing(i, acc.at[below, lo, :, :, c], came_down[i].at[lo], ydev[2])
     for i in (0, 2):
-        c, came = cut[i], wide[i]
-        for copy in by_y[i]:
+        c, one, two = cut[i], on_up[i], on_down[i]
+        by_y[i][0].wait()
+
+        def add_up(n, _):
+            acc[up, n, :, :, c] += one[n]
+            return 0
+
+        lax.fori_loop(0, 4, add_up, 0)
+        passing(i, acc.at[up, lo, :, :, c], came_up[i].at[lo], ydev[0])
+        by_y[i][1].wait()
+
+        def add_down(n, _):
+            acc[below, 4 + n, :, :, c] += two[n]
+            return 0
+
+        lax.fori_loop(0, 4, add_down, 0)
+        passing(i, acc.at[below, hi, :, :, c], came_down[i].at[hi], ydev[2])
+    for i in (0, 2):
+        c, one, two = cut[i], came_up[i], came_down[i]
+        for copy in by_y[i][2:]:
             copy.wait()
 
         def add_y(n, _):
-            acc[y, n, :, :, c] += came[0, n] + came[1, n] + came[2, n]
+            acc[y, n, :, :, c] += one[n] + two[n]
             return 0
 
         lax.fori_loop(0, Z, add_y, 0)
@@ -553,7 +605,7 @@
 
     lax.fori_loop(0, Y, add_z, 0)
     by_y[1] = [
-        remote(acc.at[lax.rem(y + k, Y), z, :, :, c], low_y.at[k - 1], ys.at[2 + k], yr.at[2 + k], ydev[k - 1])
+        remote(acc.at[lax.rem(y + k, Y), z, :, :, c], low_y.at[k - 1], ys.at[11 + k], yr.at[11 + k], ydev[k - 1])
         for k in range(1, Y)
     ]
     for i in (0, 2):
@@ -632,12 +684,12 @@
         + [
             pltpu.VMEM((Y, Z, 2, 2, SHARD, LANES), F32),
             pltpu.VMEM((Y, Z, 2, 2, SHARD, LANES), F32),
-            pltpu.VMEM((3, Z, 2, 2, 24, LANES), F32), pltpu.VMEM((3, Z, 2, 2, 16, LANES), F32),
+            *(pltpu.VMEM((n, 2, 2, rows, LANES), F32) for rows in (24, 16) for n in (4, 4, Z, Z)),
             pltpu.VMEM((3, Z, 24, LANES), F32), pltpu.VMEM((3, Z, 16, LANES), F32),
             pltpu.VMEM((7, 24, LANES), F32), pltpu.VMEM((7, 16, LANES), F32),
             pltpu.VMEM((7, Y, 2, 2, 8, LANES), F32), pltpu.VMEM((3, 2, 2, 8, LANES), F32), pltpu.VMEM((3, 8, LANES), F32),
             dma(2, 2), dma(2, 2, 2), dma(2), dma(2),
-            dma(3), dma(3), dma(9), dma(9), dma(9), dma(9), dma(21), dma(21), dma(5),
+            dma(3), dma(3), dma(15), dma(15), dma(9), dma(9), dma(21), dma(21), dma(5),
         ],
         compiler_params=pltpu.CompilerParams(collective_id=1, has_side_effects=True, vmem_limit_bytes=LIMIT),
         name="exchange_gradients",
@@ -645,47 +697,61 @@
 
 
 def update_kernel(
-    left, left_state, left_sum, right, right_state, right_sum, rel, rel_state, rel_grad,
-    left_next, left_state_next, right_next, right_state_next, rel_next, rel_state_next,
+    left_hbm, left_state, left_sum_hbm, right_hbm, right_state, right_sum_hbm, rel, rel_state, rel_grad,
+    left_next_hbm, left_state_next, right_next_hbm, right_state_next, rel_next, rel_state_next,
+    left, left_sum, left_next, right, right_sum, right_next, in_sems, out_sems,
 ):
-    for table, state, total, after, state_after in (
-        (left, left_state, left_sum, left_next, left_state_next),
-        (right, right_state, right_sum, right_next, right_state_next),
-    ):
-        grad = total[...]
-        fresh = state[...] + jnp.sum(grad * grad, axis=0, keepdims=True) * (1.0 / D)
-        state_after[...] = fresh
-        after[...] = table[...] - grad * (RATE / jnp.sqrt(fresh))
-
-    @pl.when(pl.program_id(0) == 0)
-    def _():
-        n = rel.shape[0]
-        same = lax.broadcasted_iota(I32, (n, n), 0) == lax.broadcasted_iota(I32, (n, n), 1)
-        column = lambda row: jnp.sum(jnp.where(same, jnp.broadcast_to(row, (n, n)), 0.0), axis=1, keepdims=True)
-        across = lambda col: jnp.sum(jnp.where(same, jnp.broadcast_to(col, (n, n)), 0.0), axis=0, keepdims=True)
-        grad = [rel_grad[pl.ds(j, n, stride=4), :] for j in range(4)]
-        square = jnp.sum(sum(v * v for v in grad), axis=1, keepdims=True) * (1.0 / D)
-        fresh = column(rel_state[...]) + square
-        rel_state_next[...] = across(fresh)
-        scale = RATE / jnp.sqrt(fresh)
-        for j, change in enumerate(natural_of([v * scale for v in grad])):
-            cols = pl.ds(j * LANES, change.shape[1])
-            rel_next[:, cols] = rel[:, cols] - change
+    wide = 2 * LANES
+    parts = [pl.ds(g * wide, wide) for g in range(E_PART // wide)]
+    sides = (
+        (left_hbm, left_sum_hbm, left_next_hbm, left, left_sum, left_next, left_state, left_state_next),
+        (right_hbm, right_sum_hbm, right_next_hbm, right, right_sum, right_next, right_state, right_state_next),
+    )
+    loads, stores = [], []
+    for i, side in enumerate(sides):
+        for g, at in enumerate(parts):
+            loads.append([
+                pltpu.make_async_copy(side[k].at[:, at], side[3 + k].at[:, at], in_sems.at[i, g, k]) for k in range(2)
+            ])
+            for copy in loads[-1]:
+                copy.start()
+    n = rel.shape[0]
+    same = lax.broadcasted_iota(I32, (n, n), 0) == lax.broadcasted_iota(I32, (n, n), 1)
+    column = lambda row: jnp.sum(jnp.where(same, jnp.broadcast_to(row, (n, n)), 0.0), axis=1, keepdims=True)
+    across = lambda col: jnp.sum(jnp.where(same, jnp.broadcast_to(col, (n, n)), 0.0), axis=0, keepdims=True)
+    grad = [rel_grad[pl.ds(j, n, stride=4), :] for j in range(4)]
+    square = jnp.sum(sum(v * v for v in grad), axis=1, keepdims=True) * (1.0 / D)
+    fresh = column(rel_state[...]) + square
+    rel_state_next[...] = across(fresh)
+    scale = RATE / jnp.sqrt(fresh)
+    for j, change in enumerate(natural_of([v * scale for v in grad])):
+        cols = pl.ds(j * LANES, change.shape[1])
+        rel_next[:, cols] = rel[:, cols] - change
+    for i, (_, _, after_hbm, table, total, after, state, state_after) in enumerate(sides):
+        for g, at in enumerate(parts):
+            for copy in loads[i * len(parts) + g]:
+                copy.wait()
+            grad = total[:, at]
+            fresh = state[:, at] + jnp.sum(grad * grad, axis=0, keepdims=True) * (1.0 / D)
+            state_after[:, at] = fresh
+            after[:, at] = table[:, at] - grad * (RATE / jnp.sqrt(fresh))
+            stores.append(pltpu.make_async_copy(after.at[:, at], after_hbm.at[:, at], out_sems.at[i, g]))
+            stores[-1].start()
+    for copy in stores:
+        copy.wait()
 
 
 def update(left, left_state, left_sum, right, right_state, right_sum, rel, rel_state, rel_grad):
-    wide = 2 * LANES
-    table = pl.BlockSpec((D, wide), lambda g: (0, g))
-    state = pl.BlockSpec((1, wide), lambda g: (0, g))
-    whole = lambda shape: pl.BlockSpec(shape, lambda g: (0, 0))
     shape = jax.ShapeDtypeStruct
     big, row = shape((D, E_PART), F32), shape((1, E_PART), F32)
+    side = [HBM, VMEM, HBM]
     return pl.pallas_call(
         update_kernel,
-        grid=(E_PART // wide,),
         out_shape=(big, row, big, row, shape(rel.shape, F32), shape(rel_state.shape, F32)),
-        in_specs=[table, state, table] * 2 + [whole(rel.shape), whole(rel_state.shape), whole((SHARD, LANES))],
-        out_specs=(table, state, table, state, whole(rel.shape), whole(rel_state.shape)),
+        in_specs=side * 2 + [VMEM] * 3,
+        out_specs=(HBM, VMEM, HBM, VMEM, VMEM, VMEM),
+        scratch_shapes=[pltpu.VMEM((D, E_PART), F32)] * 6
+        + [pltpu.SemaphoreType.DMA((2, 4, 2)), pltpu.SemaphoreType.DMA((2, 4))],
         compiler_params=pltpu.CompilerParams(vmem_limit_bytes=LIMIT),
         name="adagrad",
     )(left, left_state, left_sum, right, right_state, right_sum, rel, rel_state, rel_grad)
@@ -696,7 +762,7 @@
     sources, relations, targets, bucket_counts, negatives,
 ):
     left, right = left_table.T, right_table.T
-    rels, src, rel, dst, neg, counted, left_use, right_use = gather(
+    rels, src, rel, dst, neg, counted, spot, left_use, right_use = gather(
         rel_table, sources, relations, targets, negatives, bucket_counts, left, right
     )
     n_dom = 4 * Y * Z
@@ -704,8 +770,6 @@
     held, held_state, rels = lax.optimization_barrier((right_table, right_state, rels))
     held = lax.ppermute(held, "dom", route)
     held_state = lax.ppermute(held_state, "dom", route)
-    core = lax.rem(lax.axis_index("dom"), 2)
-    spot = jnp.stack([core, (core == lax.axis_index("rep")).astype(I32)])
     left_grad, right_grad, rel_grad = compute(
         spot, counted, src, rel, dst, neg, left, right, left_use, right_use, rels.reshape(-1, LANES)
     )

time: 168 us -> 164 us (0.976)
  Pallas kernels: 163 us -> 157 us
    pallas_call x1, Pallas kernels: 77.9 us -> 70.2 us  [exchange(): pl.pallas_call(exchange_kernel, out_shape=(table, table, shape((SHARD, LA...]
    pallas_call x1, Pallas kernels: 36.2 us -> 42.2 us  [compute(): pl.pallas_call(compute_kernel, out_shape=(shape((D, E_PART), F32), shape(...]
    pallas_call x1, Pallas kernels: 43.5 us -> 38.8 us  [gather(): pl.pallas_call(gather_kernel, out_shape=(shape((Y, Z, 2, 2, 2, SHARD, LAN...]
  transfers between devices with their start and end apart: 2 -> 2, of which waited for: 0 -> 0; matrix products, arithmetic and copies ran while one was open for 0% -> 0% of each run, Pallas kernels for 68% -> 69%
where the time goes in v4:
time: 164 us; the launch traced here: 162 us
  Pallas kernels  157 us (96%)
  starting transfers between devices  2.06 us (1%)
    pallas_call x1, Pallas kernels, exchange(): pl.pallas_call(exchange_kernel, out_shape=(table, table, shape((SHARD, LA...  70.2 us
    pallas_call x1, Pallas kernels, compute(): pl.pallas_call(compute_kernel, out_shape=(shape((D, E_PART), F32), shape(...  42.2 us
    pallas_call x1, Pallas kernels, gather(): pl.pallas_call(gather_kernel, out_shape=(shape((Y, Z, 2, 2, 2, SHARD, LAN...  38.8 us
    pallas_call x1, Pallas kernels, update(): pl.pallas_call(update_kernel, out_shape=(big, row, big, row, shape(rel.sh...  6.2 us
  transfers between devices with their start and end apart: 2, of which 0 were waited for; matrix products, arithmetic and copies ran while one was open for 0% of the time, Pallas kernels for 69%

profile of v4, /device:TPU:2, one launch (start us, length us, event | category | flops | bytes accessed | tf_op | source)
XLA Modules:
  0.0 162.0 jit_solution(575083349121612655)
XLA Ops:
  1.3 0.0 copy-start.3
  1.3 0.0 copy-start
  1.3 38.8 %gather_relations.1 = (f32[4,8,2,2,2,48,128]{6,5,4,3,2,1,0:T(8,128)}, s32[8192]{0:T(1024)}, s32[8192]{0:T(1024)}, s32[8192]{0:T(1024)}, s32[16,1024]{1,0:T(8,128...) custom-call(f32[12,400]{1,0:T(8,128)} %rel.3, s32[4096]{0:T(1024)} %src.1, ...), custom_call_target="tpu_custom_call" | custom-call | tf_op jit(solution)/shard_map/gather_relations/pallas_call | solution.py:231
  40.1 0.0 copy-done.3
  40.1 0.5 collective-permute-start.1
  40.6 0.0 copy-done
  40.6 1.6 collective-permute-start
  42.2 42.2 %blocks.1 = (f32[400,1024]{1,0:T(8,128)}, f32[400,1024]{1,0:T(8,128)}, f32[12288,128]{1,0:T(8,128)}) custom-call(s32[8,128]{1,0:T(8,128)} %get-tuple-element.30.spot, s32[8,128]{1,0:T(8,128)} %get-tuple-element.31.counted, s32[8192]{0:T(1024)} %get-tuple-element.32.src_hbm, s32[8192]{0:T(1024)} %get-tuple-element.33.rel_hbm, ...), custom_call_target="tpu_custom_call" | custom-call | flops 20000000000 | bytes 100000000 | tf_op jit(solution)/shard_map/blocks/pallas_call | solution.py:437
  84.4 70.2 %exchange_gradients.1 = (f32[400,1024]{1,0:T(8,128)}, f32[400,1024]{1,0:T(8,128)}, f32[48,128]{1,0:T(8,128)}) custom-call(f32[400,1024]{1,0:T(8,128)} %get-tuple-element.40.left_grad, f32[400,1024]{1,0:T(8,128)} %get-tuple-element.41.right_grad, f32[4,8,2,2,2,48,128]{6,5,4,3,2,1,0:T(8,128)} %bitcast.16), custom_call_target="tpu_custom_call" | custom-call | tf_op jit(solution)/shard_map/exchange_gradients/pallas_call | solution.py:678
  154.6 0.0 collective-permute-done.1
  154.6 0.0 copy-start.2
  154.6 0.0 collective-permute-done
  154.6 0.0 copy-start.1
  154.6 0.6 copy-done.2
  155.2 0.6 copy-done.1
  155.8 6.2 %adagrad.1 = (f32[400,1024]{1,0:T(8,128)}, f32[1,1024]{1,0:T(1,128)}, f32[400,1024]{1,0:T(8,128)}, f32[1,1024]{1,0:T(1,128)}, f32[12,400]{1,0:T(8,128)}, /*index=5*/f32[1,12]{1,0:T(1,128)}) custom-call(f32[400,1024]{1,0:T(8,128)} %bitcast.15, f32[1,1024]{1,0:T(1,128)} %bitcast.20, f32[400,1024]{1,0:T(8,128)} %get-tuple-element.43.left_sum_hbm, ...), custom_call_target="tpu_custom_call" | custom-call | tf_op jit(solution)/shard_map/adagrad/pallas_call | solution.py:748
Async XLA Ops:
  1.3 38.8 %copy-start.3 = (f32[1024]{0:T(1024)S(1)}, f32[1024]{0:T(1024)}, u32[]{:S(2)}) copy-start(f32[1024]{0:T(1024)} %param.14) | copy-start | bytes 12292
  1.3 39.3 %copy-start = (f32[1024,400]{0,1:T(8,128)S(1)}, f32[1024,400]{0,1:T(8,128)}, u32[]{:S(2)}) copy-start(f32[1024,400]{0,1:T(8,128)} %param.13) | copy-start | bytes 4915204
  40.1 114.5 %collective-permute-start.1 = (f32[1024]{0:T(1024)S(1)}, f32[1024]{0:T(1024)S(1)}, u32[]{:S(2)}, u32[]{:S(2)}) collective-permute-start(f32[1024]{0:T(1024)S(1)} %copy-done.3), channel_id=1, source_target_pairs={{254,0},{0,2},{2,4},{4,6},{6,8},{8,10},{10,12},{12,14},{14,16},{16... | collective-permute-start | bytes 12296 | tf_op jit(solution)/shard_map/ppermute | solution.py:772
  40.6 114.0 %collective-permute-start = (f32[1024,400]{0,1:T(8,128)S(1)}, f32[1024,400]{0,1:T(8,128)S(1)}, u32[]{:S(2)}, u32[]{:S(2)}) collective-permute-start(f32[1024,400]{0,1:T(8,128)S(1)} %copy-done), channel_id=1, source_target_pairs={{254,0},{0,2},{2,4},{4,6},{6,8},{8,10},{10,12},{12,14},{14,16},{16... | collective-permute-start | bytes 4915208 | tf_op jit(solution)/shard_map/ppermute | solution.py:771
  154.6 0.6 copy-start.2
  154.6 1.2 copy-start.1

commit v5 on v4

--- a/solution.py
+++ b/solution.py
@@ -17,7 +17,7 @@
 VMEM = pl.BlockSpec(memory_space=pltpu.VMEM)
 SMEM = pl.BlockSpec(memory_space=pltpu.SMEM)
 HBM = pl.BlockSpec(memory_space=pltpu.HBM)
-LIMIT = 60 * 2**20
+LIMIT = 63 * 2**20
 
 
 def tiles_of(ref, first, n):
@@ -316,7 +316,7 @@
             right_low[pl.ds(first, LANES), pl.ds(j * LANES, LANES)] = tile.astype(BF16)
         return 0
 
-    lax.fori_loop(0, E_PART // LANES, prepare, 0)
+    lax.fori_loop(0, E_PART // LANES, prepare, 0, unroll=True)
     loads[2].wait()
     unroll = 32
 
@@ -416,7 +416,7 @@
             )
         return 0
 
-    lax.fori_loop(0, E_PART // LANES, finish, 0)
+    lax.fori_loop(0, E_PART // LANES, finish, 0, unroll=True)
     outs = [
         pltpu.make_async_copy(left_turned, left_hbm_grad, sems.at[0]),
         pltpu.make_async_copy(right_turned, right_hbm_grad, sems.at[1]),
@@ -481,6 +481,13 @@
 
     pl.semaphore_wait(barrier, len(peers) + 2 * xl)
 
+    cut = [pl.ds(0, 24), pl.ds(24, 8), pl.ds(32, 16)]
+    down = [
+        remote(rel_grad.at[:, :, :, 1 - core, :, c], from_core.at[:, :, :, :, c], cs.at[i], cr.at[i], sib)
+        for i, c in enumerate(cut)
+    ]
+    keep_rel = pltpu.make_async_copy(rel_grad.at[:, :, :, core], acc, local.at[2])
+    keep_rel.start()
     half = D // 2
     mine, other = pl.ds(core * half, half), pl.ds((1 - core) * half, half)
     pairs = []
@@ -488,45 +495,6 @@
         keep = pltpu.make_async_copy(grad.at[mine], own, local.at[i])
         keep.start()
         pairs.append((remote(grad.at[other], recv, ss.at[i], sr.at[i], sib), keep))
-    cut = [pl.ds(0, 24), pl.ds(24, 8), pl.ds(32, 16)]
-    down = [
-        remote(rel_grad.at[:, :, :, 1 - core, :, c], from_core.at[:, :, :, :, c], cs.at[i], cr.at[i], sib)
-        for i, c in enumerate(cut)
-    ]
-    keep_rel = pltpu.make_async_copy(rel_grad.at[:, :, :, core], acc, local.at[2])
-    keep_rel.start()
-
-    left_to = pair + xl
-    right_to = lax.rem(pair + xl + 1, n_dom)
-    sends, stays = [], []
-    for i, (own, recv, out, to) in enumerate(
-        ((left_own, left_sib, left_sum, left_to), (right_own, right_sib, right_sum, right_to))
-    ):
-        for copy in pairs[i]:
-            copy.wait()
-
-        def add(j, _):
-            at = pl.ds(pl.multiple_of(8 * j, 8), 8)
-            own[at, :] += recv[at, :]
-            return 0
-
-        lax.fori_loop(0, half // 8, add, 0)
-        part = out.at[mine]
-        far = prepared(own, part, ls.at[i, 0], lr.at[i, core, 0], {"dom": to, "rep": 1 - xl})
-        near = prepared(own, part, ls.at[i, 1], lr.at[i, core, 1], {"dom": to, "rep": xl})
-        stay = pltpu.make_async_copy(own, part, local.at[3 + i])
-        far.start()
-        self_too = to == dom
-
-        @pl.when(self_too)
-        def _():
-            stay.start()
-
-        @pl.when(jnp.logical_not(self_too))
-        def _():
-            near.start()
-
-        sends.append((far, near, stay, self_too))
 
     keep_rel.wait()
     by_y, by_x, by_z = {0: [], 2: []}, {}, {}
@@ -560,6 +528,38 @@
         passing(i, acc.at[far, hi, :, :, c], on_down[i], ydev[2])
         passing(i, acc.at[up, hi, :, :, c], came_up[i].at[hi], ydev[0])
         passing(i, acc.at[below, lo, :, :, c], came_down[i].at[lo], ydev[2])
+    left_to = pair + xl
+    right_to = lax.rem(pair + xl + 1, n_dom)
+    sends, stays = [], []
+    for i, (own, recv, out, to) in enumerate(
+        ((left_own, left_sib, left_sum, left_to), (right_own, right_sib, right_sum, right_to))
+    ):
+        for copy in pairs[i]:
+            copy.wait()
+
+        def add(j, _):
+            at = pl.ds(pl.multiple_of(8 * j, 8), 8)
+            own[at, :] += recv[at, :]
+            return 0
+
+        lax.fori_loop(0, half // 8, add, 0)
+        part = out.at[mine]
+        far = prepared(own, part, ls.at[i, 0], lr.at[i, core, 0], {"dom": to, "rep": 1 - xl})
+        near = prepared(own, part, ls.at[i, 1], lr.at[i, core, 1], {"dom": to, "rep": xl})
+        stay = pltpu.make_async_copy(own, part, local.at[3 + i])
+        far.start()
+        self_too = to == dom
+
+        @pl.when(self_too)
+        def _():
+            stay.start()
+
+        @pl.when(jnp.logical_not(self_too))
+        def _():
+            near.start()
+
+        sends.append((far, near, stay, self_too))
+
     for i in (0, 2):
         c, one, two = cut[i], on_up[i], on_down[i]
         by_y[i][0].wait()
@@ -697,61 +697,47 @@
 
 
 def update_kernel(
-    left_hbm, left_state, left_sum_hbm, right_hbm, right_state, right_sum_hbm, rel, rel_state, rel_grad,
-    left_next_hbm, left_state_next, right_next_hbm, right_state_next, rel_next, rel_state_next,
-    left, left_sum, left_next, right, right_sum, right_next, in_sems, out_sems,
+    left, left_state, left_sum, right, right_state, right_sum, rel, rel_state, rel_grad,
+    left_next, left_state_next, right_next, right_state_next, rel_next, rel_state_next,
 ):
-    wide = 2 * LANES
-    parts = [pl.ds(g * wide, wide) for g in range(E_PART // wide)]
-    sides = (
-        (left_hbm, left_sum_hbm, left_next_hbm, left, left_sum, left_next, left_state, left_state_next),
-        (right_hbm, right_sum_hbm, right_next_hbm, right, right_sum, right_next, right_state, right_state_next),
-    )
-    loads, stores = [], []
-    for i, side in enumerate(sides):
-        for g, at in enumerate(parts):
-            loads.append([
-                pltpu.make_async_copy(side[k].at[:, at], side[3 + k].at[:, at], in_sems.at[i, g, k]) for k in range(2)
-            ])
-            for copy in loads[-1]:
-                copy.start()
-    n = rel.shape[0]
-    same = lax.broadcasted_iota(I32, (n, n), 0) == lax.broadcasted_iota(I32, (n, n), 1)
-    column = lambda row: jnp.sum(jnp.where(same, jnp.broadcast_to(row, (n, n)), 0.0), axis=1, keepdims=True)
-    across = lambda col: jnp.sum(jnp.where(same, jnp.broadcast_to(col, (n, n)), 0.0), axis=0, keepdims=True)
-    grad = [rel_grad[pl.ds(j, n, stride=4), :] for j in range(4)]
-    square = jnp.sum(sum(v * v for v in grad), axis=1, keepdims=True) * (1.0 / D)
-    fresh = column(rel_state[...]) + square
-    rel_state_next[...] = across(fresh)
-    scale = RATE / jnp.sqrt(fresh)
-    for j, change in enumerate(natural_of([v * scale for v in grad])):
-        cols = pl.ds(j * LANES, change.shape[1])
-        rel_next[:, cols] = rel[:, cols] - change
-    for i, (_, _, after_hbm, table, total, after, state, state_after) in enumerate(sides):
-        for g, at in enumerate(parts):
-            for copy in loads[i * len(parts) + g]:
-                copy.wait()
-            grad = total[:, at]
-            fresh = state[:, at] + jnp.sum(grad * grad, axis=0, keepdims=True) * (1.0 / D)
-            state_after[:, at] = fresh
-            after[:, at] = table[:, at] - grad * (RATE / jnp.sqrt(fresh))
-            stores.append(pltpu.make_async_copy(after.at[:, at], after_hbm.at[:, at], out_sems.at[i, g]))
-            stores[-1].start()
-    for copy in stores:
-        copy.wait()
+    for table, state, total, after, state_after in (
+        (left, left_state, left_sum, left_next, left_state_next),
+        (right, right_state, right_sum, right_next, right_state_next),
+    ):
+        grad = total[...]
+        fresh = state[...] + jnp.sum(grad * grad, axis=0, keepdims=True) * (1.0 / D)
+        state_after[...] = fresh
+        after[...] = table[...] - grad * (RATE / jnp.sqrt(fresh))
+
+    @pl.when(pl.program_id(0) == 0)
+    def _():
+        n = rel.shape[0]
+        same = lax.broadcasted_iota(I32, (n, n), 0) == lax.broadcasted_iota(I32, (n, n), 1)
+        column = lambda row: jnp.sum(jnp.where(same, jnp.broadcast_to(row, (n, n)), 0.0), axis=1, keepdims=True)
+        across = lambda col: jnp.sum(jnp.where(same, jnp.broadcast_to(col, (n, n)), 0.0), axis=0, keepdims=True)
+        grad = [rel_grad[pl.ds(j, n, stride=4), :] for j in range(4)]
+        square = jnp.sum(sum(v * v for v in grad), axis=1, keepdims=True) * (1.0 / D)
+        fresh = column(rel_state[...]) + square
+        rel_state_next[...] = across(fresh)
+        scale = RATE / jnp.sqrt(fresh)
+        for j, change in enumerate(natural_of([v * scale for v in grad])):
+            cols = pl.ds(j * LANES, change.shape[1])
+            rel_next[:, cols] = rel[:, cols] - change
 
 
 def update(left, left_state, left_sum, right, right_state, right_sum, rel, rel_state, rel_grad):
+    wide = 4 * LANES
+    table = pl.BlockSpec((D, wide), lambda g: (0, g))
+    state = pl.BlockSpec((1, wide), lambda g: (0, g))
+    whole = lambda shape: pl.BlockSpec(shape, lambda g: (0, 0))
     shape = jax.ShapeDtypeStruct
     big, row = shape((D, E_PART), F32), shape((1, E_PART), F32)
-    side = [HBM, VMEM, HBM]
     return pl.pallas_call(
         update_kernel,
+        grid=(E_PART // wide,),
         out_shape=(big, row, big, row, shape(rel.shape, F32), shape(rel_state.shape, F32)),
-        in_specs=side * 2 + [VMEM] * 3,
-        out_specs=(HBM, VMEM, HBM, VMEM, VMEM, VMEM),
-        scratch_shapes=[pltpu.VMEM((D, E_PART), F32)] * 6
-        + [pltpu.SemaphoreType.DMA((2, 4, 2)), pltpu.SemaphoreType.DMA((2, 4))],
+        in_specs=[table, state, table] * 2 + [whole(rel.shape), whole(rel_state.shape), whole((SHARD, LANES))],
+        out_specs=(table, state, table, state, whole(rel.shape), whole(rel_state.shape)),
         compiler_params=pltpu.CompilerParams(vmem_limit_bytes=LIMIT),
         name="adagrad",
     )(left, left_state, left_sum, right, right_state, right_sum, rel, rel_state, rel_grad)
@@ -773,6 +759,7 @@
     left_grad, right_grad, rel_grad = compute(
         spot, counted, src, rel, dst, neg, left, right, left_use, right_use, rels.reshape(-1, LANES)
     )
+    held, held_state, rel_grad = lax.optimization_barrier((held, held_state, rel_grad))
     left_sum, right_sum, rel_mine = exchange(
         left_grad, right_grad, rel_grad.reshape(Y, Z, 2, 2, 2, SHARD, LANES)
     )

time: 164 us -> 158 us (0.963)
  Pallas kernels: 157 us -> 153 us
    pallas_call x1, Pallas kernels: 42.2 us -> 35.6 us  [compute(): pl.pallas_call(compute_kernel, out_shape=(shape((D, E_PART), F32), shape(...]
    pallas_call x1, Pallas kernels: 70.2 us -> 74.3 us  [exchange(): pl.pallas_call(exchange_kernel, out_shape=(table, table, shape((SHARD, LA...]
    pallas_call x1, Pallas kernels: 6.2 us -> 4.46 us  [update(): pl.pallas_call(update_kernel, grid=(E_PART // wide,), out_shape=(big, row...]
  transfers between devices with their start and end apart: 2 -> 2, of which waited for: 0 -> 0; matrix products, arithmetic and copies ran while one was open for 0% -> 0% of each run, Pallas kernels for 69% -> 23%
where the time goes in v5:
time: 158 us; the launch traced here: 157 us
  Pallas kernels  153 us (97%)
  starting transfers between devices  2.06 us (1%)
    pallas_call x1, Pallas kernels, exchange(): pl.pallas_call(exchange_kernel, out_shape=(table, table, shape((SHARD, LA...  74.3 us
    pallas_call x1, Pallas kernels, gather(): pl.pallas_call(gather_kernel, out_shape=(shape((Y, Z, 2, 2, 2, SHARD, LAN...  38.7 us
    pallas_call x1, Pallas kernels, compute(): pl.pallas_call(compute_kernel, out_shape=(shape((D, E_PART), F32), shape(...  35.6 us
    pallas_call x1, Pallas kernels, update(): pl.pallas_call(update_kernel, grid=(E_PART // wide,), out_shape=(big, row...  4.46 us
  transfers between devices with their start and end apart: 2, of which 0 were waited for; matrix products, arithmetic and copies ran while one was open for 0% of the time, Pallas kernels for 23%

profile of v5, /device:TPU:2, one launch (start us, length us, event | category | flops | bytes accessed | tf_op | source)
XLA Modules:
  0.0 156.5 jit_solution(16944931603363309685)
XLA Ops:
  1.3 0.0 copy-start.1
  1.3 38.7 %gather_relations.1 = (f32[4,8,2,2,2,48,128]{6,5,4,3,2,1,0:T(8,128)}, s32[8192]{0:T(1024)}, s32[8192]{0:T(1024)}, s32[8192]{0:T(1024)}, s32[16,1024]{1,0:T(8,128...) custom-call(f32[12,400]{1,0:T(8,128)} %rel.3, s32[4096]{0:T(1024)} %src.1, ...), custom_call_target="tpu_custom_call" | custom-call | tf_op jit(solution)/shard_map/gather_relations/pallas_call | solution.py:231
  40.0 0.0 copy-done.1
  40.0 0.5 collective-permute-start.1
  40.5 1.6 %collective-permute-start = (f32[1024,400]{0,1:T(8,128)}, f32[1024,400]{0,1:T(8,128)}, u32[]{:S(2)}, u32[]{:S(2)}) collective-permute-start(f32[1024,400]{0,1:T(8,128)} %param.13), channel_id=1, source_target_pairs={{254,0},{0,2},{2,4},{4,6},{6,8},{8,10},{10,12},{12,14},{14,16},{16... | collective-permute-start | bytes 4915208 | tf_op jit(solution)/shard_map/ppermute | solution.py:757
  42.1 35.6 %blocks.1 = (f32[400,1024]{1,0:T(8,128)}, f32[400,1024]{1,0:T(8,128)}, f32[12288,128]{1,0:T(8,128)}) custom-call(s32[8,128]{1,0:T(8,128)} %get-tuple-element.33.spot, s32[8,128]{1,0:T(8,128)} %get-tuple-element.34.counted, s32[8192]{0:T(1024)} %get-tuple-element.35.src_hbm, s32[8192]{0:T(1024)} %get-tuple-element.36.rel_hbm, ...), custom_call_target="tpu_custom_call" | custom-call | flops 20000000000 | bytes 100000000 | tf_op jit(solution)/shard_map/blocks/pallas_call | solution.py:437
  77.7 0.0 collective-permute-done.1
  77.8 0.0 copy-start
  77.8 0.0 collective-permute-done
  77.8 74.3 %exchange_gradients.1 = (f32[400,1024]{1,0:T(8,128)}, f32[400,1024]{1,0:T(8,128)}, f32[48,128]{1,0:T(8,128)}) custom-call(f32[400,1024]{1,0:T(8,128)} %get-tuple-element.43.left_grad, f32[400,1024]{1,0:T(8,128)} %get-tuple-element.44.right_grad, f32[4,8,2,2,2,48,128]{6,5,4,3,2,1,0:T(8,128)} %bitcast.16), custom_call_target="tpu_custom_call" | custom-call | tf_op jit(solution)/shard_map/exchange_gradients/pallas_call | solution.py:678
  152.1 0.0 copy-done
  152.1 4.5 %adagrad.1 = (f32[400,1024]{1,0:T(8,128)}, f32[1,1024]{1,0:T(1,128)}, f32[400,1024]{1,0:T(8,128)}, f32[1,1024]{1,0:T(1,128)}, f32[12,400]{1,0:T(8,128)}, /*index=5*/f32[1,12]{1,0:T(1,128)}) custom-call(f32[400,1024]{1,0:T(8,128)} %bitcast.15, f32[1,1024]{1,0:T(1,128)} %bitcast.19, f32[400,1024]{1,0:T(8,128)} %get-tuple-element.49.left_sum, ...), custom_call_target="tpu_custom_call" | custom-call | tf_op jit(solution)/shard_map/adagrad/pallas_call | solution.py:735
Async XLA Ops:
  1.3 38.7 %copy-start.1 = (f32[1024]{0:T(1024)S(1)}, f32[1024]{0:T(1024)}, u32[]{:S(2)}) copy-start(f32[1024]{0:T(1024)} %param.14) | copy-start | bytes 12292
  40.0 37.7 %collective-permute-start.1 = (f32[1024]{0:T(1024)S(1)}, f32[1024]{0:T(1024)S(1)}, u32[]{:S(2)}, u32[]{:S(2)}) collective-permute-start(f32[1024]{0:T(1024)S(1)} %copy-done.1), channel_id=1, source_target_pairs={{254,0},{0,2},{2,4},{4,6},{6,8},{8,10},{10,12},{12,14},{14,16},{16... | collective-permute-start | bytes 12296 | tf_op jit(solution)/shard_map/ppermute | solution.py:758
  40.5 37.3 %collective-permute-start = (f32[1024,400]{0,1:T(8,128)}, f32[1024,400]{0,1:T(8,128)}, u32[]{:S(2)}, u32[]{:S(2)}) collective-permute-start(f32[1024,400]{0,1:T(8,128)} %param.13), channel_id=1, source_target_pairs={{254,0},{0,2},{2,4},{4,6},{6,8},{8,10},{10,12},{12,14},{14,16},{16... | collective-permute-start | bytes 4915208 | tf_op jit(solution)/shard_map/ppermute | solution.py:757
  77.8 74.3 %copy-start = (f32[1024]{0:T(1024)}, f32[1024]{0:T(1024)S(1)}, u32[]{:S(2)}) copy-start(f32[1024]{0:T(1024)S(1)} %collective-permute-done.1) | copy-start | bytes 12292

commit v6 on v5

--- a/solution.py
+++ b/solution.py
@@ -270,7 +270,7 @@
     spot, counted, src_hbm, rel_hbm, dst_hbm, neg, left_here, right_here, left_sent, right_sent, rels_hbm,
     left_hbm_grad, right_hbm_grad, rel_hbm_grad,
     left, right, rels, left_turned, right_turned, left_grad, right_grad, rel_grad,
-    left_rows, right_rows, right_low, low_turned, heads, relat, tails, q_low, prob, neg_t, src, rel, dst, ids_in, sems, id_sems,
+    left_rows, right_rows, right_low, heads, relat, tails, q_low, prob, neg_t, src, rel, dst, ids_in, sems, id_sems,
 ):
     count, core, at_home = counted[0, 0], spot[0, 0], spot[1, 0]
     n_blocks = (((count + GROUP - 1) >> 9) + 1 - core) >> 1
@@ -310,7 +310,6 @@
         for j, tile in enumerate(embedding_tiles(left, g)):
             left_rows[pl.ds(4 * first + j, LANES, stride=4), :] = tile.T
         for j, tile in enumerate(embedding_tiles(right, g)):
-            low_turned[pl.ds(j * LANES, LANES), pl.ds(first, LANES)] = tile.astype(BF16)
             tile = tile.T
             right_rows[pl.ds(4 * first + j, LANES, stride=4), :] = tile
             right_low[pl.ds(first, LANES), pl.ds(j * LANES, LANES)] = tile.astype(BF16)
@@ -362,7 +361,9 @@
             positive = jnp.sum(q[0] * t[0] + q[1] * t[1] + q[2] * t[2] + q[3] * t[3], axis=1, keepdims=True)
             ql = jnp.concatenate([x.astype(BF16) for x in q], axis=1)
             q_low[rows, :] = ql
-            scores = jnp.dot(ql, low_turned[...], preferred_element_type=F32) + bias
+            scores = lax.dot_general(
+                ql, right_low[...], (((1,), (1,)), ((), ())), preferred_element_type=F32
+            ) + bias
             place_in = b * GROUP + ch * CHUNK + lax.broadcasted_iota(I32, (CHUNK, 1), 0)
             live = (place_in < count).astype(F32)
             top = jnp.maximum(positive, jnp.max(scores, axis=1, keepdims=True))
@@ -405,23 +406,18 @@
     rel_out = pltpu.make_async_copy(rel_grad, rel_hbm_grad, sems.at[2])
     rel_out.start()
 
-    def finish(g, _):
-        first = pl.multiple_of(g * LANES, LANES)
-        to = pl.ds(first, LANES)
-        for j, (start, size) in enumerate(((0, 128), (128, 72), (200, 128), (328, 72))):
-            at = pl.ds(4 * first + j, LANES, stride=4)
-            left_turned[pl.ds(start, size), to] = left_grad[at, :].T[:size]
-            right_turned[pl.ds(start, size), to] = (
-                right_grad[at, :].T[:size] + neg_t[pl.ds(j * LANES, size), to]
-            )
-        return 0
-
-    lax.fori_loop(0, E_PART // LANES, finish, 0, unroll=True)
     outs = [
         pltpu.make_async_copy(left_turned, left_hbm_grad, sems.at[0]),
         pltpu.make_async_copy(right_turned, right_hbm_grad, sems.at[1]),
     ]
-    for copy in outs:
+    for grad, turned, copy in ((left_grad, left_turned, outs[0]), (right_grad, right_turned, outs[1])):
+        for g in range(E_PART // LANES):
+            to = pl.ds(g * LANES, LANES)
+            for j, (start, size) in enumerate(((0, 128), (128, 72), (200, 128), (328, 72))):
+                part = grad[pl.ds(4 * g * LANES + j, LANES, stride=4), :].T[:size]
+                if grad is right_grad:
+                    part += neg_t[pl.ds(j * LANES, size), to]
+                turned[pl.ds(start, size), to] = part
         copy.start()
     for copy in outs:
         copy.wait()
@@ -442,7 +438,7 @@
         scratch_shapes=[
             table, table, pltpu.VMEM((n, LANES), F32), table, table, rows, rows, pltpu.VMEM((n, LANES), F32),
             rows, rows,
-            pltpu.VMEM((E_PART, 512), BF16), pltpu.VMEM((512, E_PART), BF16),
+            pltpu.VMEM((E_PART, 512), BF16),
             block, block, block,
             pltpu.VMEM((GROUP, 512), BF16), pltpu.VMEM((GROUP, E_PART), BF16), pltpu.VMEM((512, E_PART), F32),
             pltpu.SMEM((2 * SLOTS,), I32), pltpu.SMEM((2 * SLOTS,), I32), pltpu.SMEM((2 * SLOTS,), I32),

time: 158 us -> 158 us (level)
    pallas_call x1, Pallas kernels: 74.3 us -> 66.7 us  [exchange(): pl.pallas_call(exchange_kernel, out_shape=(table, table, shape((SHARD, LA...]
    pallas_call x1, Pallas kernels: 35.6 us -> 41.7 us  [compute(): pl.pallas_call(compute_kernel, out_shape=(shape((D, E_PART), F32), shape(...]
  transfers between devices with their start and end apart: 2 -> 2, of which waited for: 0 -> 0; matrix products, arithmetic and copies ran while one was open for 0% -> 0% of each run, Pallas kernels for 23% -> 27%
where the time goes in v6:
time: 158 us; the launch traced here: 155 us
  Pallas kernels  152 us (96%)
  starting transfers between devices  2.06 us (1%)
    pallas_call x1, Pallas kernels, exchange(): pl.pallas_call(exchange_kernel, out_shape=(table, table, shape((SHARD, LA...  66.7 us
    pallas_call x1, Pallas kernels, compute(): pl.pallas_call(compute_kernel, out_shape=(shape((D, E_PART), F32), shape(...  41.7 us
    pallas_call x1, Pallas kernels, gather(): pl.pallas_call(gather_kernel, out_shape=(shape((Y, Z, 2, 2, 2, SHARD, LAN...  38.7 us
    pallas_call x1, Pallas kernels, update(): pl.pallas_call(update_kernel, grid=(E_PART // wide,), out_shape=(big, row...  4.46 us
  transfers between devices with their start and end apart: 2, of which 0 were waited for; matrix products, arithmetic and copies ran while one was open for 0% of the time, Pallas kernels for 27%

profile of v6, /device:TPU:2, one launch (start us, length us, event | category | flops | bytes accessed | tf_op | source)
XLA Modules:
  0.0 155.0 jit_solution(11468241600890368797)
XLA Ops:
  1.3 0.0 copy-start.1
  1.3 38.7 %gather_relations.1 = (f32[4,8,2,2,2,48,128]{6,5,4,3,2,1,0:T(8,128)}, s32[8192]{0:T(1024)}, s32[8192]{0:T(1024)}, s32[8192]{0:T(1024)}, s32[16,1024]{1,0:T(8,128...) custom-call(f32[12,400]{1,0:T(8,128)} %rel.3, s32[4096]{0:T(1024)} %src.1, ...), custom_call_target="tpu_custom_call" | custom-call | tf_op jit(solution)/shard_map/gather_relations/pallas_call | solution.py:231
  40.0 0.0 copy-done.1
  40.0 0.5 collective-permute-start.1
  40.5 1.6 %collective-permute-start = (f32[1024,400]{0,1:T(8,128)}, f32[1024,400]{0,1:T(8,128)}, u32[]{:S(2)}, u32[]{:S(2)}) collective-permute-start(f32[1024,400]{0,1:T(8,128)} %param.13), channel_id=1, source_target_pairs={{254,0},{0,2},{2,4},{4,6},{6,8},{8,10},{10,12},{12,14},{14,16},{16... | collective-permute-start | bytes 4915208 | tf_op jit(solution)/shard_map/ppermute | solution.py:753
  42.1 41.7 %blocks.1 = (f32[400,1024]{1,0:T(8,128)}, f32[400,1024]{1,0:T(8,128)}, f32[12288,128]{1,0:T(8,128)}) custom-call(s32[8,128]{1,0:T(8,128)} %get-tuple-element.33.spot, s32[8,128]{1,0:T(8,128)} %get-tuple-element.34.counted, s32[8192]{0:T(1024)} %get-tuple-element.35.src_hbm, s32[8192]{0:T(1024)} %get-tuple-element.36.rel_hbm, ...), custom_call_target="tpu_custom_call" | custom-call | flops 20000000000 | bytes 100000000 | tf_op jit(solution)/shard_map/blocks/pallas_call | solution.py:433
  83.8 0.0 collective-permute-done.1
  83.8 0.0 copy-start
  83.8 0.0 collective-permute-done
  83.8 66.7 %exchange_gradients.1 = (f32[400,1024]{1,0:T(8,128)}, f32[400,1024]{1,0:T(8,128)}, f32[48,128]{1,0:T(8,128)}) custom-call(f32[400,1024]{1,0:T(8,128)} %get-tuple-element.43.left_grad, f32[400,1024]{1,0:T(8,128)} %get-tuple-element.44.right_grad, f32[4,8,2,2,2,48,128]{6,5,4,3,2,1,0:T(8,128)} %bitcast.16), custom_call_target="tpu_custom_call" | custom-call | tf_op jit(solution)/shard_map/exchange_gradients/pallas_call | solution.py:674
  150.5 0.0 copy-done
  150.5 4.5 %adagrad.1 = (f32[400,1024]{1,0:T(8,128)}, f32[1,1024]{1,0:T(1,128)}, f32[400,1024]{1,0:T(8,128)}, f32[1,1024]{1,0:T(1,128)}, f32[12,400]{1,0:T(8,128)}, /*index=5*/f32[1,12]{1,0:T(1,128)}) custom-call(f32[400,1024]{1,0:T(8,128)} %bitcast.15, f32[1,1024]{1,0:T(1,128)} %bitcast.19, f32[400,1024]{1,0:T(8,128)} %get-tuple-element.49.left_sum, ...), custom_call_target="tpu_custom_call" | custom-call | tf_op jit(solution)/shard_map/adagrad/pallas_call | solution.py:731
Async XLA Ops:
  1.3 38.7 %copy-start.1 = (f32[1024]{0:T(1024)S(1)}, f32[1024]{0:T(1024)}, u32[]{:S(2)}) copy-start(f32[1024]{0:T(1024)} %param.14) | copy-start | bytes 12292
  40.0 43.8 %collective-permute-start.1 = (f32[1024]{0:T(1024)S(1)}, f32[1024]{0:T(1024)S(1)}, u32[]{:S(2)}, u32[]{:S(2)}) collective-permute-start(f32[1024]{0:T(1024)S(1)} %copy-done.1), channel_id=1, source_target_pairs={{254,0},{0,2},{2,4},{4,6},{6,8},{8,10},{10,12},{12,14},{14,16},{16... | collective-permute-start | bytes 12296 | tf_op jit(solution)/shard_map/ppermute | solution.py:754
  40.5 43.3 %collective-permute-start = (f32[1024,400]{0,1:T(8,128)}, f32[1024,400]{0,1:T(8,128)}, u32[]{:S(2)}, u32[]{:S(2)}) collective-permute-start(f32[1024,400]{0,1:T(8,128)} %param.13), channel_id=1, source_target_pairs={{254,0},{0,2},{2,4},{4,6},{6,8},{8,10},{10,12},{12,14},{14,16},{16... | collective-permute-start | bytes 4915208 | tf_op jit(solution)/shard_map/ppermute | solution.py:753
  83.8 66.7 %copy-start = (f32[1024]{0:T(1024)}, f32[1024]{0:T(1024)S(1)}, u32[]{:S(2)}) copy-start(f32[1024]{0:T(1024)S(1)} %collective-permute-done.1) | copy-start | bytes 12292
